TPU v7x, 768 devices: a whole 4x8x12 slice. The times are simulated.
768 devices in a mesh: gx: 16 (over x, y_hi, core), yz: 48 (over z, y_lo).
Axes of the slice: x: 4, y: 8 (y_hi: 2, y_lo: 4; y = y_hi * 4 + y_lo), z: 12, core: 2. Of those that a mesh axis runs over, the one named last changes fastest.
Arguments:
- positions: float32 [16, 48, 3, 64], P('gx', 'yz'), may hold values from 0 to 3
- species: int32 [16, 48, 64], P('gx', 'yz'), may hold values from 0 to 5
- charges: float32 [16, 48, 64], P('gx', 'yz'), may hold values from -1 to 1
- neighbours: int32 [16, 48, 16, 64], P('gx', 'yz'), may hold values from 0 to 567
- counts: int32 [16, 48, 64], P('gx', 'yz'), may hold values from 4 to 16
- send_list: int32 [16, 48, 56], P('gx', 'yz'), may hold values from 0 to 63, as said below
- species_table: float32 [6, 128], replicated, may hold values from -6 to 6
- charge_weight: float32 [128], replicated, may hold values from -6 to 6
- w_center: bfloat16 [128, 128], replicated, may hold values from -0.5 to 0.5
- w_neigh: bfloat16 [128, 128], replicated, may hold values from -0.5 to 0.5
- w_radial: float32 [8, 128], replicated, may hold values from -4 to 4
- w_two: bfloat16 [128, 128], replicated, may hold values from -0.5 to 0.5
- w_env: bfloat16 [1, 128, 64], replicated, may hold values from -0.5 to 0.5
- w_tensor: bfloat16 [1, 128, 64], replicated, may hold values from -0.5 to 0.5
- w_latent: bfloat16 [1, 320, 128], replicated, may hold values from -0.3125 to 0.3125
- w_out: bfloat16 [128], replicated, may hold values from -0.5 to 0.5
Outputs:
- atom_energy: float32 [16, 48, 64], P('gx', 'yz')
- forces: float32 [16, 48, 3, 64], P('gx', 'yz')
Inputs may be any that keep to these rules, and one draw needn't show every extreme that they name: `send_list`: 56 distinct owned atoms of each domain.
All inputs are finite; a program needn't handle non-finite values.
Results may differ from a plain program's by a relative error of at most 0.013.
Values may be sent and summed in bfloat16 or wider, within the bound.
No kernel may reach another device: no remote copies, remote signals or barrier semaphores. Data moves between devices by JAX's collectives and lax.ppermute only.
A program may use at most 32 MiB of HBM per device.

v0:
```python
import jax
import jax.numpy as jnp
from jax import lax
from jax.sharding import PartitionSpec as P

box_side = 3.0
core_sq = 1.0
env_width = 32.0
basis_width = 0.5


def from_behind(value, axis, steps):
    count = lax.axis_size(axis)
    pairs = [(source, (source + steps) % count) for source in range(count)]
    return lax.ppermute(value, axis, pairs)


def with_halo(cells, sides, width):
    for axis, dim in sides:
        count = lax.axis_size(axis)
        head = lax.slice_in_dim(cells, 0, width, axis=dim)
        tail = lax.slice_in_dim(cells, cells.shape[dim] - width, cells.shape[dim], axis=dim)
        cells = jnp.concatenate(
            [
                lax.ppermute(tail, axis, [(i, (i + 1) % count) for i in range(count)]),
                cells,
                lax.ppermute(head, axis, [((i + 1) % count, i) for i in range(count)]),
            ],
            axis=dim,
        )
    return cells


def node_hidden(species_value, charge, species_table, charge_weight):
    kinds = jnp.arange(species_table.shape[0]).astype(species_value.dtype)
    onehot = (species_value[:, None] == kinds[None, :]).astype(species_table.dtype)
    mixed = (
        jnp.dot(onehot, species_table, precision=lax.Precision.HIGHEST)
        + charge[:, None] * charge_weight[None, :]
    )
    return jax.nn.silu(mixed).astype(jnp.bfloat16)


def gaussian_basis(distance, count):
    centres = 1.0 + jnp.arange(count).astype(distance.dtype)
    spread = distance[:, None] - centres[None, :]
    return jnp.exp(-spread * spread / basis_width)


def harmonics(direction):
    along_x, along_y, along_z = (direction[0], direction[1], direction[2])
    square = along_x * along_x + along_y * along_y + along_z * along_z
    return jnp.stack(
        [
            jnp.ones_like(along_x),
            along_x,
            along_y,
            along_z,
            along_x * along_y,
            along_y * along_z,
            along_x * along_z,
            along_x * along_x - along_y * along_y,
            3.0 * along_z * along_z - square,
        ]
    )


def atom_energies(
    own_pos,
    ghost_pos,
    center,
    neigh_all,
    neighbour_ids,
    counts,
    w_radial,
    w_two,
    w_env,
    w_tensor,
    w_latent,
    w_out,
):
    neigh_count = neighbour_ids.shape[0]
    atom_count = own_pos.shape[1]
    blocks = jnp.arange(9)
    shift_x = (blocks // 3 - 1).astype(own_pos.dtype) * box_side
    shift_y = (blocks % 3 - 1).astype(own_pos.dtype) * box_side
    offset = jnp.stack([shift_x, shift_y, jnp.zeros_like(shift_x)], axis=1)
    placed = ghost_pos + offset[:, :, None]
    ghosts = jnp.transpose(placed, (1, 0, 2)).reshape(3, -1)
    every_pos = jnp.concatenate([own_pos, ghosts], axis=1)
    flat_ids = neighbour_ids.reshape(-1)
    far_pos = jnp.take(every_pos, flat_ids, axis=1)
    near_pos = jnp.tile(own_pos, (1, neigh_count))
    offset_vec = far_pos - near_pos
    distance = jnp.sqrt(jnp.sum(offset_vec * offset_vec, axis=0) + core_sq)
    direction = offset_vec / distance[None, :]
    harmonic = harmonics(direction)
    envelope = jnp.exp(-distance * distance / env_width)
    slot_index = jnp.arange(neigh_count)[:, None]
    in_list = (slot_index < counts[None, :]).astype(own_pos.dtype).reshape(-1)
    weight_edge = envelope * in_list
    radial_basis = gaussian_basis(distance, w_radial.shape[0])
    pair_sum = jnp.tile(center, (neigh_count, 1)) + jnp.take(neigh_all, flat_ids, axis=0).astype(
        center.dtype
    )
    pair_sum = pair_sum + jnp.dot(radial_basis, w_radial, precision=lax.Precision.HIGHEST)
    first_latent = jax.nn.silu(pair_sum).astype(jnp.bfloat16)
    latent = jax.nn.silu(jnp.dot(first_latent, w_two, preferred_element_type=jnp.float32))
    harmonic_grid = harmonic.reshape(9, neigh_count, atom_count)
    latent_bf = latent.astype(jnp.bfloat16)
    env_weight = (
        jnp.dot(latent_bf, w_env[0], preferred_element_type=jnp.float32) * weight_edge[:, None]
    )
    channel = jnp.dot(latent_bf, w_tensor[0], preferred_element_type=jnp.float32)
    env_grid = env_weight.reshape(neigh_count, atom_count, -1)
    summed = 0.25 * jnp.einsum(
        "kac,mka->mca", env_grid, harmonic_grid, precision=lax.Precision.HIGHEST
    )
    pieces = []
    for start_m, stop_m in ((0, 1), (1, 4), (4, 9)):
        pieces.append(
            jnp.einsum(
                "mka,mca->kac",
                harmonic_grid[start_m:stop_m],
                summed[start_m:stop_m],
                precision=lax.Precision.HIGHEST,
            )
        )
    grouped = jnp.concatenate(pieces, axis=-1).reshape(neigh_count * atom_count, -1)
    scalars = (grouped * jnp.tile(channel, (1, 3))).astype(jnp.bfloat16)
    joined = jnp.concatenate([latent_bf, scalars], axis=1)
    latent = latent + jax.nn.silu(jnp.dot(joined, w_latent[0], preferred_element_type=jnp.float32))
    out_bf = latent.astype(jnp.bfloat16)
    edge_energy = jnp.dot(out_bf, w_out, preferred_element_type=jnp.float32) * weight_edge
    return jnp.sum(edge_energy.reshape(neigh_count, atom_count), axis=0)


def send_along_yz(blocks, step):
    return from_behind(blocks, "yz", step)


def send_along_gx(blocks, step):
    return from_behind(blocks, "gx", step)


def local(
    positions,
    species,
    charges,
    neighbours,
    counts,
    send_list,
    species_table,
    charge_weight,
    w_center,
    w_neigh,
    w_radial,
    w_two,
    w_env,
    w_tensor,
    w_latent,
    w_out,
):
    own_pos = positions[0, 0]
    species_value = species[0, 0].astype(jnp.float32)
    charge = charges[0, 0]
    neighbour_ids = neighbours[0, 0]
    live_counts = counts[0, 0]
    sends = send_list[0, 0]
    ghost_count = sends.shape[0]
    hidden_own = node_hidden(species_value, charge, species_table, charge_weight)
    center = jnp.dot(hidden_own, w_center, preferred_element_type=jnp.float32)
    neigh = jnp.dot(hidden_own, w_neigh, preferred_element_type=jnp.float32).astype(jnp.bfloat16)
    send_pos = jnp.take(own_pos, sends, axis=1)
    ghost_grid = with_halo(send_pos[None, None], (("gx", 0), ("yz", 1)), 1)
    ghost_pos = ghost_grid.reshape(9, 3, ghost_count)
    send_neigh = jnp.take(neigh, sends, axis=0)
    neigh_grid = with_halo(send_neigh[None, None], (("gx", 0), ("yz", 1)), 1)
    ghost_neigh = neigh_grid.reshape(9 * ghost_count, -1)
    neigh_all = jnp.concatenate([neigh, ghost_neigh], axis=0)

    def energy_of(own_value, ghost_value):
        return atom_energies(
            own_value,
            ghost_value,
            center,
            neigh_all,
            neighbour_ids,
            live_counts,
            w_radial,
            w_two,
            w_env,
            w_tensor,
            w_latent,
            w_out,
        )

    energies, pullback = jax.vjp(energy_of, own_pos, ghost_pos)
    grad_own, grad_ghost = pullback(jnp.ones_like(energies))
    ghost_blocks = grad_ghost.reshape(3, 3, 3, ghost_count)
    column_sum = (
        ghost_blocks[:, 1]
        + send_along_yz(ghost_blocks[:, 2], 1)
        + send_along_yz(ghost_blocks[:, 0], -1)
    )
    returned = column_sum[1] + send_along_gx(column_sum[2], 1) + send_along_gx(column_sum[0], -1)
    total = grad_own.at[:, sends].add(returned)
    return (energies[None, None], (-total)[None, None])


def solution(mesh):
    return jax.shard_map(
        local,
        mesh=mesh,
        in_specs=(
            P("gx", "yz", None, None),
            P("gx", "yz", None),
            P("gx", "yz", None),
            P("gx", "yz", None, None),
            P("gx", "yz", None),
            P("gx", "yz", None),
            P(),
            P(),
            P(),
            P(),
            P(),
            P(),
            P(),
            P(),
            P(),
            P(),
        ),
        out_specs=(P("gx", "yz", None), P("gx", "yz", None, None)),
        check_vma=False,
    )
```

profile of v0, /device:TPU:39, one launch (start us, length us, event | category | flops | bytes accessed | tf_op | source)
XLA Modules:
  0.0 149.7 jit_solution(8673597873884909204)
XLA Ops:
  6.0 2.6 %collective-permute-start.1 = (bf16[1,1,56,128]{3,2,1,0:T(8,128)(2,1)S(1)}, bf16[1,1,56,128]{3,2,1,0:T(8,128)(2,1)S(1)}, u32[]{:S(2)}, u32[]{:S(2)}) collective-permute-start(bf16[1,1,56,128]{3,2,1,0:T(8,128)(2,1)S(1)} %bitcast_select_fusion.1), channel_id=1, source_target_pairs={{48,0},{96,48},{144,96},{192,144},{240,192},{288,240},{336,288},{3... | collective-permute-start | bytes 43016 | tf_op jit(solution)/shard_map/ppermute | solution.py:27
  8.6 10.6 %collective-permute-start = (bf16[1,1,56,128]{3,2,1,0:T(8,128)(2,1)S(1)}, bf16[1,1,56,128]{3,2,1,0:T(8,128)(2,1)S(1)}, u32[]{:S(2)}, u32[]{:S(2)}) collective-permute-start(bf16[1,1,56,128]{3,2,1,0:T(8,128)(2,1)S(1)} %bitcast_select_fusion.1), channel_id=1, source_target_pairs={{0,48},{48,96},{96,144},{144,192},{192,240},{240,288},{288,336},{3... | collective-permute-start | bytes 43016 | tf_op jit(solution)/shard_map/ppermute | solution.py:25
  20.6 1.9 %collective-permute-start.5 = (f32[1,1,3,56]{2,3,1,0:T(8,128)S(1)}, f32[1,1,3,56]{2,3,1,0:T(8,128)S(1)}, u32[]{:S(2)}, u32[]{:S(2)}) collective-permute-start(f32[1,1,3,56]{2,3,1,0:T(8,128)S(1)} %bitcast_select_fusion), channel_id=1, source_target_pairs={{48,0},{96,48},{144,96},{192,144},{240,192},{288,240},{336,288},{3... | collective-permute-start | bytes 2024 | tf_op jit(solution)/shard_map/ppermute | solution.py:27
  22.5 9.7 %collective-permute-start.4 = (f32[1,1,3,56]{2,3,1,0:T(8,128)S(1)}, f32[1,1,3,56]{2,3,1,0:T(8,128)S(1)}, u32[]{:S(2)}, u32[]{:S(2)}) collective-permute-start(f32[1,1,3,56]{2,3,1,0:T(8,128)S(1)} %bitcast_select_fusion), channel_id=1, source_target_pairs={{0,48},{48,96},{96,144},{144,192},{192,240},{240,288},{288,336},{3... | collective-permute-start | bytes 2024 | tf_op jit(solution)/shard_map/ppermute | solution.py:25
  35.4 13.1 %collective-permute-start.7 = (f32[3,1,3,56]{2,3,1,0:T(8,128)S(1)}, f32[3,1,3,56]{2,3,1,0:T(8,128)S(1)}, u32[]{:S(2)}, u32[]{:S(2)}) collective-permute-start(f32[3,1,3,56]{2,3,1,0:T(8,128)S(1)} %pad_maximum_fusion.4), channel_id=1, source_target_pairs={{1,0},{2,1},{3,2},{4,3},{5,4},{6,5},{7,6},{8,7},{9,8},{10,9},{11,1... | collective-permute-start | bytes 6056 | tf_op jit(solution)/shard_map/ppermute | solution.py:27
  48.5 1.9 %collective-permute-start.6 = (f32[3,1,3,56]{2,3,1,0:T(8,128)S(1)}, f32[3,1,3,56]{2,3,1,0:T(8,128)S(1)}, u32[]{:S(2)}, u32[]{:S(2)}) collective-permute-start(f32[3,1,3,56]{2,3,1,0:T(8,128)S(1)} %pad_maximum_fusion.4), channel_id=1, source_target_pairs={{0,1},{1,2},{2,3},{3,4},{4,5},{5,6},{6,7},{7,8},{8,9},{9,10},{10,1... | collective-permute-start | bytes 6056 | tf_op jit(solution)/shard_map/ppermute | solution.py:25
  50.5 1.1 convert.3
  52.1 5.5 %collective-permute-done.6 = f32[3,1,3,56]{2,3,1,0:T(8,128)S(1)} collective-permute-done((f32[3,1,3,56]{2,3,1,0:T(8,128)S(1)}, f32[3,1,3,56]{2,3,1,0:T(8,128)S(1)}, u32[]{:S(2)}, u32[]{:S(2)}) %collective-permute-start.6) | collective-permute-done | bytes 2048 | tf_op jit(solution)/shard_map/ppermute | solution.py:25
  58.0 2.8 %gather_fusion.3 = f32[1024,3]{1,0:T(8,128)S(1)} fusion(f32[3,568]{0,1:T(8,128)S(1)} %pad_maximum_fusion.1, s32[1024]{0:T(1024)S(1)} %get-tuple-element.72), kind=kCustom, calls=%fused_computation.3 | custom fusion | bytes 28672 | tf_op jit(solution)/shard_map/jvp(jit(_take))/gather | solution.py:92
  62.9 1.9 %collective-permute-start.3 = (bf16[3,1,56,128]{3,2,1,0:T(8,128)(2,1)S(1)}, bf16[3,1,56,128]{3,2,1,0:T(8,128)(2,1)S(1)}, u32[]{:S(2)}, u32[]{:S(2)}) collective-permute-start(bf16[3,1,56,128]{3,2,1,0:T(8,128)(2,1)S(1)} %pad_maximum_fusion.5), channel_id=1, source_target_pairs={{1,0},{2,1},{3,2},{4,3},{5,4},{6,5},{7,6},{8,7},{9,8},{10,9},{11,1... | collective-permute-start | bytes 129032 | tf_op jit(solution)/shard_map/ppermute | solution.py:27
  64.9 3.4 %collective-permute-start.2 = (bf16[3,1,56,128]{3,2,1,0:T(8,128)(2,1)S(1)}, bf16[3,1,56,128]{3,2,1,0:T(8,128)(2,1)S(1)}, u32[]{:S(2)}, u32[]{:S(2)}) collective-permute-start(bf16[3,1,56,128]{3,2,1,0:T(8,128)(2,1)S(1)} %pad_maximum_fusion.5), channel_id=1, source_target_pairs={{0,1},{1,2},{2,3},{3,4},{4,5},{5,6},{6,7},{7,8},{8,9},{9,10},{10,1... | collective-permute-start | bytes 129032 | tf_op jit(solution)/shard_map/ppermute | solution.py:25
  70.3 3.3 %collective-permute-done.2 = bf16[3,1,56,128]{3,2,1,0:T(8,128)(2,1)S(1)} collective-permute-done((bf16[3,1,56,128]{3,2,1,0:T(8,128)(2,1)S(1)}, bf16[3,1,56,128]{3,2,1,0:T(8,128)(2,1)S(1)}, u32[]{:S(2)}, u32[]{:S(2)}) %collective-permute-start.2) | collective-permute-done | bytes 43040 | tf_op jit(solution)/shard_map/ppermute | solution.py:25
  73.6 3.4 %gather_fusion.1 = bf16[1024,128]{1,0:T(8,128)(2,1)S(1)} fusion(bf16[568,128]{1,0:T(8,128)(2,1)S(1)} %pad_maximum_fusion.2, s32[1024]{0:T(1024)S(1)} %get-tuple-element.72), kind=kCustom, calls=%fused_computation.1 | custom fusion | bytes 528384 | tf_op jit(solution)/shard_map/jvp(jit(_take))/gather | solution.py:103
  77.2 1.1 convolution_add_fusion
  78.4 1.1 fusion.51
  81.9 1.0 fusion
  82.9 1.1 convolution_bitcast_fusion
  84.0 1.1 convolution_bitcast_fusion.1
  89.1 1.6 %convolution_bitcast_fusion.4 = f32[5,64,64]{1,0,2:T(8,128)} fusion(f32[5,16,64]{1,0,2:T(8,128)S(1)} %copy.346, f32[16,64,64]{2,1,0:T(8,128)S(1)} %get-tuple-element.32), kind=kOutput, calls=%fused_computation.25 | convolution fusion | flops 3932160 | bytes 364544 | tf_op jit(solution)/shard_map/transpose(jvp(mka,mca->kac))/dot_general | solution.py:122
  90.7 1.9 %convolution_bitcast_fusion.5 = f32[5,16,64]{1,0,2:T(8,128)} fusion(f32[16,64,64]{2,1,0:T(8,128)S(1)} %get-tuple-element.32, f32[9,64,64]{1,0,2:T(8,128)S(1)} %fusion), kind=kOutput, calls=%fused_computation.26 | convolution fusion | flops 3932160 | bytes 806912 | tf_op jit(solution)/shard_map/transpose(jvp(mka,mca->kac))/dot_general | solution.py:122
  93.6 1.8 %convolution_bitcast_fusion.9 = f32[1,16,64]{1,0,2:T(1,128)} fusion(f32[64,64,16]{1,0,2:T(8,128)S(1)} %get-tuple-element.33, f32[9,64,64]{1,0,2:T(8,128)S(1)} %fusion), kind=kOutput, calls=%fused_computation.33 | convolution fusion | flops 786432 | bytes 561152 | tf_op jit(solution)/shard_map/transpose(jvp(mka,mca->kac))/dot_general | solution.py:122
  95.4 1.1 convolution_bitcast_fusion.6
  96.5 1.2 convolution_bitcast_fusion.7
  97.8 1.0 fusion.43
  100.1 1.9 %fusion.1 = f32[9,16,64]{1,0,2:T(8,128)S(1)} fusion(f32[16,64,64]{2,0,1:T(8,128)S(1)} %copy.344, f32[1,16,64]{1,0,2:T(1,128)} %convolution_bitcast_fusion.9, f32[3,16,64]{1,0,2:T(4,128)S(1)} %convolution_bitcast_fusion.7, f32[5,16,64]{1,0,2:T(8,128)S(1)} %copy-done.6, f32[1,64,64]{1,0,2:T(1,128)S(1)} %convolution_bitcast_fusion.8, ...), kind=kOutput, calls=%fused_computation.16 | convolution fusion | flops 7216128 | bytes 483328 | tf_op jit(solution)/shard_map/transpose(jvp(kac,mka->mca))/dot_general | solution.py:116
  105.2 1.5 %fusion.2 = f32[1024,128]{1,0:T(8,128)S(1)} fusion(bf16[128,128]{1,0:T(8,128)(2,1)S(1)} %copy-done.29, f32[1024,128]{1,0:T(8,128)S(1)} %copy-done.34, bf16[1024,128]{1,0:T(8,128)(2,1)S(1)} %convolution_convert_fusion.2, bf16[1024,64]{0,1:T(8,128)(2,1)S(1)} %reduce_sum.64, bf16[1024,320]{1,0:T(8,128)(2,1)} %copy-done.9, f32[128]{0:T(128)S(1)} %copy-done.32, ...), kind=kOutput, calls=%fused_computation.18 | convolution fusion | flops 53084160 | bytes 1757696 | tf_op jit(solution)/shard_map/transpose(jvp())/dot_general | solution.py:108
  109.0 6.2 %scatter_custom_fusion = f32[3,568]{0,1:T(8,128)S(1)} fusion(s32[1024]{0:T(1024)} %bitcast.204, f32[1024,3]{1,0:T(8,128)S(1)} %copy.370, f32[]{:T(128)} %constant.107.clone.1), kind=kCustom, calls=%fused_computation.91 | custom fusion | flops 3072 | bytes 7328 | tf_op jit(solution)/shard_map/transpose(jvp(jit(_take)))/scatter-add | solution.py:92
  115.4 1.9 %collective-permute-start.8 = (f32[3,3,56]{2,1,0:T(4,128)S(1)}, f32[3,3,56]{2,1,0:T(4,128)S(1)}, u32[]{:S(2)}, u32[]{:S(2)}) collective-permute-start(f32[3,3,56]{2,1,0:T(4,128)S(1)} %get-tuple-element.48), channel_id=1, source_target_pairs={{0,1},{1,2},{2,3},{3,4},{4,5},{5,6},{6,7},{7,8},{8,9},{9,10},{10,1... | collective-permute-start | bytes 6056 | tf_op jit(solution)/shard_map/ppermute | solution.py:15
  117.3 7.3 %collective-permute-start.9 = (f32[3,3,56]{2,1,0:T(4,128)S(1)}, f32[3,3,56]{2,1,0:T(4,128)S(1)}, u32[]{:S(2)}, u32[]{:S(2)}) collective-permute-start(f32[3,3,56]{2,1,0:T(4,128)S(1)} %get-tuple-element.49), channel_id=1, source_target_pairs={{0,47},{1,0},{2,1},{3,2},{4,3},{5,4},{6,5},{7,6},{8,7},{9,8},{10,9... | collective-permute-start | bytes 6056 | tf_op jit(solution)/shard_map/ppermute | solution.py:15
  125.4 11.8 %collective-permute-start.10 = (f32[3,56]{1,0:T(4,128)S(1)}, f32[3,56]{1,0:T(4,128)S(1)}, u32[]{:S(2)}, u32[]{:S(2)}) collective-permute-start(f32[3,56]{1,0:T(4,128)S(1)} %get-tuple-element.58), channel_id=1, source_target_pairs={{0,48},{48,96},{96,144},{144,192},{192,240},{240,288},{288,336},{3... | collective-permute-start | bytes 2024 | tf_op jit(solution)/shard_map/ppermute | solution.py:15
  137.1 1.9 %collective-permute-start.11 = (f32[3,56]{1,0:T(4,128)S(1)}, f32[3,56]{1,0:T(4,128)S(1)}, u32[]{:S(2)}, u32[]{:S(2)}) collective-permute-start(f32[3,56]{1,0:T(4,128)S(1)} %get-tuple-element.59), channel_id=1, source_target_pairs={{0,720},{48,0},{96,48},{144,96},{192,144},{240,192},{288,240},{336... | collective-permute-start | bytes 2024 | tf_op jit(solution)/shard_map/ppermute | solution.py:15
  139.7 8.4 %collective-permute-done.11 = f32[3,56]{1,0:T(4,128)S(1)} collective-permute-done((f32[3,56]{1,0:T(4,128)S(1)}, f32[3,56]{1,0:T(4,128)S(1)}, u32[]{:S(2)}, u32[]{:S(2)}) %collective-permute-start.11) | collective-permute-done | bytes 704 | tf_op jit(solution)/shard_map/ppermute | solution.py:15
  (210 shorter events, 32.1 us)
Async XLA Ops:
  0.6 85.6 %copy-start = (bf16[1,320,128]{2,1,0:T(8,128)(2,1)S(1)}, bf16[1,320,128]{2,1,0:T(8,128)(2,1)}, u32[]{:S(2)}) copy-start(bf16[1,320,128]{2,1,0:T(8,128)(2,1)} %param.30) | copy-start | bytes 245764
  1.3 4.0 %copy-start.23 = (s32[56]{0:T(128)}, s32[56]{0:T(128)S(1)}, u32[]{:S(2)}) copy-start(s32[56]{0:T(128)S(1)} %fusion.107) | copy-start | bytes 676
  3.4 1.8 %copy-start.17 = (s32[1024,1]{0,1:T(1,128)}, s32[1024,1]{0,1:T(1,128)S(1)}, u32[]{:S(2)}) copy-start(s32[1024,1]{0,1:T(1,128)S(1)} %compare_select_fusion) | copy-start | bytes 12292
  6.0 56.9 %collective-permute-start.1 = (bf16[1,1,56,128]{3,2,1,0:T(8,128)(2,1)S(1)}, bf16[1,1,56,128]{3,2,1,0:T(8,128)(2,1)S(1)}, u32[]{:S(2)}, u32[]{:S(2)}) collective-permute-start(bf16[1,1,56,128]{3,2,1,0:T(8,128)(2,1)S(1)} %bitcast_select_fusion.1), channel_id=1, source_target_pairs={{48,0},{96,48},{144,96},{192,144},{240,192},{288,240},{336,288},{3... | collective-permute-start | bytes 43016 | tf_op jit(solution)/shard_map/ppermute | solution.py:27
  8.6 54.3 %collective-permute-start = (bf16[1,1,56,128]{3,2,1,0:T(8,128)(2,1)S(1)}, bf16[1,1,56,128]{3,2,1,0:T(8,128)(2,1)S(1)}, u32[]{:S(2)}, u32[]{:S(2)}) collective-permute-start(bf16[1,1,56,128]{3,2,1,0:T(8,128)(2,1)S(1)} %bitcast_select_fusion.1), channel_id=1, source_target_pairs={{0,48},{48,96},{96,144},{144,192},{192,240},{240,288},{288,336},{3... | collective-permute-start | bytes 43016 | tf_op jit(solution)/shard_map/ppermute | solution.py:25
  20.6 14.8 %collective-permute-start.5 = (f32[1,1,3,56]{2,3,1,0:T(8,128)S(1)}, f32[1,1,3,56]{2,3,1,0:T(8,128)S(1)}, u32[]{:S(2)}, u32[]{:S(2)}) collective-permute-start(f32[1,1,3,56]{2,3,1,0:T(8,128)S(1)} %bitcast_select_fusion), channel_id=1, source_target_pairs={{48,0},{96,48},{144,96},{192,144},{240,192},{288,240},{336,288},{3... | collective-permute-start | bytes 2024 | tf_op jit(solution)/shard_map/ppermute | solution.py:27
  22.5 12.9 %collective-permute-start.4 = (f32[1,1,3,56]{2,3,1,0:T(8,128)S(1)}, f32[1,1,3,56]{2,3,1,0:T(8,128)S(1)}, u32[]{:S(2)}, u32[]{:S(2)}) collective-permute-start(f32[1,1,3,56]{2,3,1,0:T(8,128)S(1)} %bitcast_select_fusion), channel_id=1, source_target_pairs={{0,48},{48,96},{96,144},{144,192},{192,240},{240,288},{288,336},{3... | collective-permute-start | bytes 2024 | tf_op jit(solution)/shard_map/ppermute | solution.py:25
  35.4 16.6 %collective-permute-start.7 = (f32[3,1,3,56]{2,3,1,0:T(8,128)S(1)}, f32[3,1,3,56]{2,3,1,0:T(8,128)S(1)}, u32[]{:S(2)}, u32[]{:S(2)}) collective-permute-start(f32[3,1,3,56]{2,3,1,0:T(8,128)S(1)} %pad_maximum_fusion.4), channel_id=1, source_target_pairs={{1,0},{2,1},{3,2},{4,3},{5,4},{6,5},{7,6},{8,7},{9,8},{10,9},{11,1... | collective-permute-start | bytes 6056 | tf_op jit(solution)/shard_map/ppermute | solution.py:27
  48.5 9.1 %collective-permute-start.6 = (f32[3,1,3,56]{2,3,1,0:T(8,128)S(1)}, f32[3,1,3,56]{2,3,1,0:T(8,128)S(1)}, u32[]{:S(2)}, u32[]{:S(2)}) collective-permute-start(f32[3,1,3,56]{2,3,1,0:T(8,128)S(1)} %pad_maximum_fusion.4), channel_id=1, source_target_pairs={{0,1},{1,2},{2,3},{3,4},{4,5},{5,6},{6,7},{7,8},{8,9},{9,10},{10,1... | collective-permute-start | bytes 6056 | tf_op jit(solution)/shard_map/ppermute | solution.py:25
  50.4 26.8 %copy-start.26 = (f32[8]{0:T(128)}, f32[8]{0:T(128)S(1)}, u32[]{:S(2)}) copy-start(f32[8]{0:T(128)S(1)} %convert_add_fusion) | copy-start | bytes 100
  50.5 10.7 %copy-start.25 = (s32[1,1,64]{2,1,0:T(1,128)S(1)}, s32[1,1,64]{2,1,0:T(1,128)}, u32[]{:S(2)}) copy-start(s32[1,1,64]{2,1,0:T(1,128)} %param.20) | copy-start | bytes 772
  51.9 9.3 %copy-start.18 = (pred[1024]{0:T(1024)(128)(4,1)}, pred[1024]{0:T(1024)(128)(4,1)S(1)}, u32[]{:S(2)}) copy-start(pred[1024]{0:T(1024)(128)(4,1)S(1)} %lt.104) | copy-start | bytes 3076
  61.2 7.7 %copy-start.11 = (f32[3,1024]{1,0:T(4,128)}, f32[3,1024]{1,0:T(4,128)S(1)}, u32[]{:S(2)}) copy-start(f32[3,1024]{1,0:T(4,128)S(1)} %get-tuple-element.30) | copy-start | bytes 36868
  62.9 7.3 %collective-permute-start.3 = (bf16[3,1,56,128]{3,2,1,0:T(8,128)(2,1)S(1)}, bf16[3,1,56,128]{3,2,1,0:T(8,128)(2,1)S(1)}, u32[]{:S(2)}, u32[]{:S(2)}) collective-permute-start(bf16[3,1,56,128]{3,2,1,0:T(8,128)(2,1)S(1)} %pad_maximum_fusion.5), channel_id=1, source_target_pairs={{1,0},{2,1},{3,2},{4,3},{5,4},{6,5},{7,6},{8,7},{9,8},{10,9},{11,1... | collective-permute-start | bytes 129032 | tf_op jit(solution)/shard_map/ppermute | solution.py:27
  64.9 8.7 %collective-permute-start.2 = (bf16[3,1,56,128]{3,2,1,0:T(8,128)(2,1)S(1)}, bf16[3,1,56,128]{3,2,1,0:T(8,128)(2,1)S(1)}, u32[]{:S(2)}, u32[]{:S(2)}) collective-permute-start(bf16[3,1,56,128]{3,2,1,0:T(8,128)(2,1)S(1)} %pad_maximum_fusion.5), channel_id=1, source_target_pairs={{0,1},{1,2},{2,3},{3,4},{4,5},{5,6},{6,7},{7,8},{8,9},{9,10},{10,1... | collective-permute-start | bytes 129032 | tf_op jit(solution)/shard_map/ppermute | solution.py:25
  73.6 3.6 %copy-start.20 = (f32[8,128]{1,0:T(8,128)S(1)}, f32[8,128]{1,0:T(8,128)}, u32[]{:S(2)}) copy-start(f32[8,128]{1,0:T(8,128)} %param.26) | copy-start | bytes 12292
  81.9 2.1 %copy-start.2 = (f32[3,16,64]{1,0,2:T(4,128)S(1)}, f32[3,16,64]{1,0,2:T(4,128)}, u32[]{:S(2)}) copy-start(f32[3,16,64]{1,0,2:T(4,128)} %copy.345) | copy-start | bytes 36868
  95.4 2.4 %copy-start.30 = (bf16[128]{0:T(256)(128)(2,1)S(1)}, bf16[128]{0:T(256)(128)(2,1)}, u32[]{:S(2)}) copy-start(bf16[128]{0:T(256)(128)(2,1)} %param.31) | copy-start | bytes 772
  95.4 2.4 %copy-start.33 = (f32[1024,128]{1,0:T(8,128)S(1)}, f32[1024,128]{1,0:T(8,128)}, u32[]{:S(2)}) copy-start(f32[1024,128]{1,0:T(8,128)} %get-tuple-element.66) | copy-start | bytes 1572868
  100.0 2.1 %copy-start.10 = (f32[16,64]{0,1:T(8,128)S(1)}, f32[16,64]{0,1:T(8,128)}, u32[]{:S(2)}) copy-start(f32[16,64]{0,1:T(8,128)} %copy.366) | copy-start | bytes 12292
  103.0 1.9 %copy-start.14 = (bf16[1,128,64]{1,2,0:T(8,128)(2,1)S(1)}, bf16[1,128,64]{1,2,0:T(8,128)(2,1)}, u32[]{:S(2)}) copy-start(bf16[1,128,64]{1,2,0:T(8,128)(2,1)} %param.28) | copy-start | bytes 49156
  103.0 2.1 %copy-start.16 = (bf16[1,128,64]{1,2,0:T(8,128)(2,1)S(1)}, bf16[1,128,64]{1,2,0:T(8,128)(2,1)}, u32[]{:S(2)}) copy-start(bf16[1,128,64]{1,2,0:T(8,128)(2,1)} %param.29) | copy-start | bytes 49156
  103.0 2.1 %copy-start.29 = (bf16[128,128]{1,0:T(8,128)(2,1)S(1)}, bf16[128,128]{1,0:T(8,128)(2,1)}, u32[]{:S(2)}) copy-start(bf16[128,128]{1,0:T(8,128)(2,1)} %param.27) | copy-start | bytes 98308
  103.0 2.1 %copy-start.32 = (f32[128]{0:T(128)S(1)}, f32[128]{0:T(128)}, u32[]{:S(2)}) copy-start(f32[128]{0:T(128)} %convert.3) | copy-start | bytes 1540
  103.1 2.1 %copy-start.34 = (f32[1024,128]{1,0:T(8,128)S(1)}, f32[1024,128]{1,0:T(8,128)}, u32[]{:S(2)}) copy-start(f32[1024,128]{1,0:T(8,128)} %get-tuple-element.66) | copy-start | bytes 1572868
  105.2 1.6 %copy-start.8 = (f32[1024,128]{1,0:T(8,128)S(1)}, f32[1024,128]{1,0:T(8,128)}, u32[]{:S(2)}) copy-start(f32[1024,128]{1,0:T(8,128)} %copy-done.7) | copy-start | bytes 1572868
  105.2 1.6 %copy-start.21 = (f32[8,128]{1,0:T(8,128)S(1)}, f32[8,128]{1,0:T(8,128)}, u32[]{:S(2)}) copy-start(f32[8,128]{1,0:T(8,128)} %param.26) | copy-start | bytes 12292
  108.6 39.5 %copy-start.24 = (s32[56]{0:T(128)S(1)}, s32[56]{0:T(128)}, u32[]{:S(2)}) copy-start(s32[56]{0:T(128)} %copy-done.23) | copy-start | bytes 676
  115.4 9.4 %collective-permute-start.8 = (f32[3,3,56]{2,1,0:T(4,128)S(1)}, f32[3,3,56]{2,1,0:T(4,128)S(1)}, u32[]{:S(2)}, u32[]{:S(2)}) collective-permute-start(f32[3,3,56]{2,1,0:T(4,128)S(1)} %get-tuple-element.48), channel_id=1, source_target_pairs={{0,1},{1,2},{2,3},{3,4},{4,5},{5,6},{6,7},{7,8},{8,9},{9,10},{10,1... | collective-permute-start | bytes 6056 | tf_op jit(solution)/shard_map/ppermute | solution.py:15
  117.3 8.0 %collective-permute-start.9 = (f32[3,3,56]{2,1,0:T(4,128)S(1)}, f32[3,3,56]{2,1,0:T(4,128)S(1)}, u32[]{:S(2)}, u32[]{:S(2)}) collective-permute-start(f32[3,3,56]{2,1,0:T(4,128)S(1)} %get-tuple-element.49), channel_id=1, source_target_pairs={{0,47},{1,0},{2,1},{3,2},{4,3},{5,4},{6,5},{7,6},{8,7},{9,8},{10,9... | collective-permute-start | bytes 6056 | tf_op jit(solution)/shard_map/ppermute | solution.py:15
  125.4 14.3 %collective-permute-start.10 = (f32[3,56]{1,0:T(4,128)S(1)}, f32[3,56]{1,0:T(4,128)S(1)}, u32[]{:S(2)}, u32[]{:S(2)}) collective-permute-start(f32[3,56]{1,0:T(4,128)S(1)} %get-tuple-element.58), channel_id=1, source_target_pairs={{0,48},{48,96},{96,144},{144,192},{192,240},{240,288},{288,336},{3... | collective-permute-start | bytes 2024 | tf_op jit(solution)/shard_map/ppermute | solution.py:15
  137.1 10.9 %collective-permute-start.11 = (f32[3,56]{1,0:T(4,128)S(1)}, f32[3,56]{1,0:T(4,128)S(1)}, u32[]{:S(2)}, u32[]{:S(2)}) collective-permute-start(f32[3,56]{1,0:T(4,128)S(1)} %get-tuple-element.59), channel_id=1, source_target_pairs={{0,720},{48,0},{96,48},{144,96},{192,144},{240,192},{288,240},{336... | collective-permute-start | bytes 2024 | tf_op jit(solution)/shard_map/ppermute | solution.py:15
  (15 other events, 15.0 us)
where the time goes:
time: 151 us; the launch traced here: 150 us
  starting transfers between devices  67.9 us (45%)
  matrix products  24.8 us (16%)
  local copies, waits for them, and re-layouts  23.2 us (15%)
  waiting for transfers between devices  17.7 us (12%)
  other arithmetic  14.5 us (10%)
  between operations  1.62 us (1%)
    ppermute x4, starting transfers between devices, with_halo(): lax.ppermute(tail, axis, [(i, (i + 1) % count) for i in range(count)])  25.5 us
    ppermute x4, starting transfers between devices, from_behind(): return lax.ppermute(value, axis, pairs)  22.9 us
    ppermute x4, starting transfers between devices, with_halo(): lax.ppermute(head, axis, [((i + 1) % count, i) for i in range(count)])  19.5 us
    dot_general x8, matrix products, atom_energies(): jnp.einsum('mka,mca->kac', harmonic_grid[start_m:stop_m], summed[start_m:...  10.7 us
    ppermute x4, waiting for transfers between devices, from_behind(): return lax.ppermute(value, axis, pairs)  8.92 us
    ppermute x4, waiting for transfers between devices, with_halo(): lax.ppermute(tail, axis, [(i, (i + 1) % count) for i in range(count)])  8.78 us
    scatter-add x1, other arithmetic, atom_energies(): far_pos = jnp.take(every_pos, flat_ids, axis=1)  6.21 us
    unnamed x77, local copies, waits for them, and re-layouts  4.89 us
  transfers between devices with their start and end apart: 12, of which 4 were waited for; matrix products, arithmetic and copies ran while one was open for 10% of the time, Pallas kernels for 0%

commit v1 on v0

v1 whole, which is shorter than its diff:
```python
import jax
import jax.numpy as jnp
from jax import lax
from jax.experimental import pallas as pl
from jax.experimental.pallas import tpu as pltpu
from jax.sharding import PartitionSpec as P

box_side = 3.0
f32 = jnp.float32
bf16 = jnp.bfloat16


def groups_of(shift):
    slabs, columns = lax.axis_size("gx"), lax.axis_size("yz")
    return [
        [
            (2 * m + shift + a) % slabs * columns + (2 * n + shift + b) % columns
            for a in (0, 1)
            for b in (0, 1)
        ]
        for m in range(slabs // 2)
        for n in range(columns // 2)
    ]


def swap(value, shift):
    return lax.all_to_all(value, ("gx", "yz"), 0, 0, axis_index_groups=groups_of(shift))


def halves(value):
    high = lax.reduce_precision(value, 8, 7)
    return high, lax.reduce_precision(value - high, 8, 7)


def thirds(value):
    high, mid = halves(value)
    return high, mid, lax.reduce_precision(value - high - mid, 8, 7)


def mm(a, b):
    return jnp.dot(a, b, preferred_element_type=f32)


def half_turn(x):
    return x + pltpu.roll(x, 64, 1)


def sigmoid(x):
    return 0.5 * jnp.tanh(0.5 * x) + 0.5


def edge_kernel(
    blocks_ref,
    nb_ref,
    count_ref,
    w_kind_ref,
    w_pair_ref,
    w_center_t_ref,
    w_two_t_ref,
    w_ec_t_ref,
    w_lat_t_ref,
    w_two_ref,
    w_back_ref,
    w_scal_ref,
    w_rad_ref,
    w_out_row_ref,
    cols_ref,
    grad_ref,
    energy_ref,
    lat_ref,
    ds1_ref,
    ds2_ref,
    lb_ref,
    er_ref,
    ch_ref,
    s_ref,
    dg_ref,
    du_ref,
    dch_ref,
    dsum_ref,
    rows_ref,
):
    odd_x = lax.rem(lax.axis_index("gx"), 2)
    odd_y = lax.rem(lax.axis_index("yz"), 2)

    def block(b):
        u = 2 - odd_x + (b // 3 - 1)
        v = 2 - odd_y + (b % 3 - 1)
        far = (u // 2) * 2 + v // 2
        near = (u % 2) * 2 + v % 2
        return blocks_ref[far, pl.ds(pl.multiple_of(near * 8, 8), 8), :]

    tables = [block(b) for b in range(9)]

    ids = jnp.concatenate([nb_ref[0:8, :], nb_ref[8:16, :]], axis=1)
    count = jnp.concatenate([count_ref[...], count_ref[...]], axis=1)
    row = lax.broadcasted_iota(jnp.int32, (8, 128), 0)
    lane = lax.broadcasted_iota(jnp.int32, (8, 128), 1)
    slot = row + jnp.where(lane >= 64, 8, 0)
    live = jnp.where(slot < count, 1.0, 0.0)
    own = ids < 64
    beyond = ids - 64
    blk = jnp.zeros_like(ids)
    for b in range(1, 9):
        blk = blk + jnp.where(beyond >= 56 * b, 1, 0)
    place = jnp.where(own, ids, beyond - 56 * blk)
    blk = jnp.where(own, 4, blk)

    def pick(which, index, start):
        out = start
        for b in range(9):
            table = jnp.broadcast_to(tables[b][which : which + 1, :], (8, 128))
            value = jnp.take_along_axis(table, index, axis=1, mode="promise_in_bounds")
            out = jnp.where(blk == b, value, out)
        return out

    listed = pick(5, place, jnp.zeros((8, 128), f32)).astype(jnp.int32)
    atom = jnp.where(own, ids, listed)
    zero = jnp.zeros((8, 128), f32)
    far_x, far_y, far_z, far_q, far_s = [pick(i, atom, zero) for i in range(5)]
    step_x = jnp.where(blk >= 6, 1, jnp.where(blk >= 3, 0, -1))
    step_y = blk - 3 * (step_x + 1) - 1
    mine = tables[4]
    off_x = far_x + box_side * step_x.astype(f32) - mine[0:1, :]
    off_y = far_y + box_side * step_y.astype(f32) - mine[1:2, :]
    off_z = far_z - mine[2:3, :]
    square = off_x * off_x + off_y * off_y + off_z * off_z + 1.0
    dist = jnp.sqrt(square)
    inv = 1.0 / dist
    x, y, z = off_x * inv, off_y * inv, off_z * inv
    harm = [
        None,
        x,
        y,
        z,
        x * y,
        y * z,
        x * z,
        x * x - y * y,
        2.0 * z * z - x * x - y * y,
    ]
    weight = jnp.exp(square * (-1.0 / 32.0)) * live

    kind_row = lax.broadcasted_iota(jnp.int32, (8, 128), 0).astype(f32)
    cw = jnp.broadcast_to(cols_ref[:, 0:1], (128, 128))
    wo = jnp.broadcast_to(cols_ref[:, 1:2], (128, 128))
    cw2 = jnp.concatenate([cw, cw], axis=1)
    wo2 = jnp.concatenate([wo, wo], axis=1)
    centres = 1.0 + lax.broadcasted_iota(jnp.int32, (8, 256), 0).astype(f32)

    def hidden(kind, charge, wide_cw, wide_row):
        onehot = jnp.where(kind == wide_row, 1.0, 0.0)
        pad = jnp.zeros_like(onehot)
        rhs = jnp.concatenate([onehot, onehot, onehot, pad], axis=0).astype(bf16)
        mixed = mm(w_kind_ref[...], rhs) + wide_cw * charge
        return mixed * sigmoid(mixed)

    center = mm(
        w_center_t_ref[...], hidden(mine[4:5, :], mine[3:4, :], cw, kind_row).astype(bf16)
    )
    center2 = jnp.concatenate([center, center], axis=1)
    kind_row2 = jnp.concatenate([kind_row, kind_row], axis=1)

    def wide(packed, c):
        return jnp.concatenate([packed[2 * c : 2 * c + 1, :], packed[2 * c + 1 : 2 * c + 2, :]], axis=1)

    def basis(c):
        spread = wide(dist, c) - centres
        return spread, jnp.exp(-2.0 * spread * spread)

    for c in range(4):
        at = slice(256 * c, 256 * c + 256)
        hid = hidden(wide(far_s, c), wide(far_q, c), cw2, kind_row2)
        _, rb = basis(c)
        rb_high = rb.astype(bf16).astype(f32)
        rhs = jnp.concatenate([hid, rb_high, rb_high, rb - rb_high, jnp.zeros_like(rb)], axis=0)
        pair = mm(w_pair_ref[...], rhs.astype(bf16)) + center2
        sig = sigmoid(pair)
        act = pair * sig
        ds1_ref[:, at] = sig + act * (1.0 - sig)
        second = mm(w_two_t_ref[...], act.astype(bf16))
        sig = sigmoid(second)
        latent = second * sig
        ds2_ref[:, at] = sig + latent * (1.0 - sig)
        lat_ref[:, at] = latent
        latent_bf = latent.astype(bf16)
        lb_ref[:, at] = latent_bf
        both = mm(w_ec_t_ref[...], latent_bf)
        er_ref[:, at] = both[:64]
        ch_ref[:, at] = both[64:]

    def row_of(packed, r):
        return packed[r : r + 1, :]

    def lanes(r):
        return slice(128 * r, 128 * r + 128)

    group_of = [0, 1, 1, 1, 2, 2, 2, 2, 2]
    weighted = [None] + [h * weight for h in harm[1:]]
    for m in range(9):
        scale = weight if m == 0 else weighted[m]
        total = er_ref[:, lanes(0)] * row_of(scale, 0)
        for r in range(1, 8):
            total = total + er_ref[:, lanes(r)] * row_of(scale, r)
        s_ref[m] = 0.25 * half_turn(total)

    def double(value):
        return jnp.concatenate([value, value], axis=1)

    def keep_row(index, c, value):
        rows_ref[index, 2 * c : 2 * c + 1, :] = value[:, :128]
        rows_ref[index, 2 * c + 1 : 2 * c + 2, :] = value[:, 128:]

    for c in range(4):
        at = slice(256 * c, 256 * c + 256)
        channel = ch_ref[:, at]
        grouped = [double(s_ref[0]), None, None]
        for m in range(1, 9):
            term = double(s_ref[m]) * wide(harm[m], c)
            g = group_of[m]
            grouped[g] = term if grouped[g] is None else grouped[g] + term
        scalars = [(g * channel).astype(bf16) for g in grouped]
        joined = jnp.concatenate([lb_ref[:, at]] + scalars, axis=0)
        update = mm(w_lat_t_ref[...], joined)
        sig = sigmoid(update)
        act = update * sig
        out_bf = (lat_ref[:, at] + act).astype(bf16)
        keep_row(0, c, mm(w_out_row_ref[...], out_bf)[0:1])
        d_update = (wo2 * wide(weight, c) * (sig + act * (1.0 - sig))).astype(bf16)
        du_ref[:, at] = d_update
        d_scal = mm(w_scal_ref[...], d_update)
        d_grouped = []
        d_channel = None
        for g in range(3):
            part = d_scal[64 * g : 64 * g + 64]
            term = part * grouped[g]
            d_channel = term if d_channel is None else d_channel + term
            d_grouped.append(part * channel)
            dg_ref[g, :, at] = d_grouped[g]
        dch_ref[:, at] = d_channel.astype(bf16)
        for m in range(1, 9):
            keep_row(m, c, jnp.sum(d_grouped[group_of[m]] * double(s_ref[m]), axis=0, keepdims=True))

    for m in range(9):
        g = group_of[m]
        total = None
        for r in range(8):
            term = dg_ref[g, :, lanes(r)]
            if m > 0:
                term = term * row_of(harm[m], r)
            total = term if total is None else total + term
        dsum_ref[m] = 0.25 * half_turn(total)

    for c in range(4):
        at = slice(256 * c, 256 * c + 256)
        raw = er_ref[:, at]
        w_row = wide(weight, c)
        d_env = double(dsum_ref[0])
        for m in range(1, 9):
            back = double(dsum_ref[m])
            d_env = d_env + back * wide(harm[m], c)
            keep_row(8 + m, c, jnp.sum(raw * back, axis=0, keepdims=True))
        keep_row(17, c, jnp.sum(raw * d_env, axis=0, keepdims=True))
        d_joined = jnp.concatenate(
            [du_ref[:, at], (d_env * w_row).astype(bf16), dch_ref[:, at]], axis=0
        )
        d_latent = mm(w_back_ref[...], d_joined) + wo2 * w_row
        d_second = (d_latent * ds2_ref[:, at]).astype(bf16)
        d_pair = mm(w_two_ref[...], d_second) * ds1_ref[:, at]
        high = d_pair.astype(bf16)
        low = (d_pair - high.astype(f32)).astype(bf16)
        first = mm(w_rad_ref[...], high)
        d_basis = first[0:8] + first[8:16] + mm(w_rad_ref[...], low)[0:8]
        spread, rb = basis(c)
        keep_row(18, c, jnp.sum(d_basis * rb * spread, axis=0, keepdims=True) * -4.0)

    energy = jnp.sum(rows_ref[0] * weight, axis=0, keepdims=True)
    energy_ref[...] = half_turn(energy)[:, :64]
    d_h = [None] + [rows_ref[m] + weight * rows_ref[8 + m] for m in range(1, 9)]
    g_x = d_h[1] + y * d_h[4] + z * d_h[6] + 2.0 * x * (d_h[7] - d_h[8])
    g_y = d_h[2] + x * d_h[4] + z * d_h[5] - 2.0 * y * (d_h[7] + d_h[8])
    g_z = d_h[3] + y * d_h[5] + x * d_h[6] + 4.0 * z * d_h[8]
    d_weight = rows_ref[0] + rows_ref[17]
    d_dist = (
        rows_ref[18]
        - inv * (g_x * x + g_y * y + g_z * z)
        - d_weight * weight * dist * (1.0 / 16.0)
    )
    e_x = g_x * inv + d_dist * x
    e_y = g_y * inv + d_dist * y
    e_z = g_z * inv + d_dist * z

    u = 1 + odd_x + step_x
    v = 1 + odd_y + step_y
    target = ((u // 2) * 2 + v // 2) * 4 + (u % 2) * 2 + v % 2
    atom_row = lax.broadcasted_iota(jnp.int32, (64, 128), 0)
    pairs_row = lax.broadcasted_iota(jnp.int32, (8, 128), 0)
    part_row = lax.rem(pairs_row, 4)
    left, right = [], []
    for r in range(8):
        mixed = jnp.where(
            part_row == 0,
            row_of(e_x, r),
            jnp.where(part_row == 1, row_of(e_y, r), jnp.where(part_row == 2, row_of(e_z, r), 0.0)),
        )
        high = mixed.astype(bf16).astype(f32)
        low = mixed - high
        goal = jnp.broadcast_to(row_of(target, r), (8, 128)) - jnp.where(pairs_row >= 4, 1, 0)
        stack = [jnp.where(goal == 2 * i, high, 0.0) for i in range(8)]
        stack += [jnp.where(goal == 2 * i, low, 0.0) for i in range(8)]
        left.append(jnp.concatenate(stack, axis=0).astype(bf16))
        right.append(jnp.where(atom_row == row_of(atom, r), 1.0, 0.0).astype(bf16))
    far = lax.dot_general(
        jnp.concatenate(left, axis=1),
        jnp.concatenate(right, axis=1),
        (((1,), (1,)), ((), ())),
        preferred_element_type=f32,
    )
    far = far[:64] + far[64:]
    near = jnp.concatenate(
        [half_turn(jnp.sum(e, axis=0, keepdims=True))[:, :64] for e in (e_x, e_y, e_z)]
        + [jnp.zeros((1, 64), f32)],
        axis=0,
    )
    near = jnp.concatenate([near, near], axis=0)
    home = ((1 + odd_x) // 2 * 2 + (1 + odd_y) // 2) * 4 + lax.rem(1 + odd_x, 2) * 2 + lax.rem(1 + odd_y, 2)
    half_row = jnp.where(lax.broadcasted_iota(jnp.int32, (8, 64), 0) >= 4, 1, 0)
    for i in range(8):
        here = far[8 * i : 8 * i + 8]
        grad_ref[i // 2, 8 * (i % 2) : 8 * (i % 2) + 8, :] = here - jnp.where(
            half_row + 2 * i == home, near, 0.0
        )


def local(
    positions,
    species,
    charges,
    neighbours,
    counts,
    send_list,
    species_table,
    charge_weight,
    w_center,
    w_neigh,
    w_radial,
    w_two,
    w_env,
    w_tensor,
    w_latent,
    w_out,
):
    sends = jnp.pad(send_list[0].astype(f32), ((0, 0), (0, 8)))
    mine = jnp.concatenate(
        [positions[0, 0], charges[0], species[0].astype(f32), sends, jnp.zeros((2, 64), f32)],
        axis=0,
    )
    mine = jnp.concatenate([mine, mine], axis=1)
    four = swap(jnp.broadcast_to(mine[None], (4, 8, 128)), 0).reshape(32, 128)
    blocks = swap(jnp.broadcast_to(four[None], (4, 32, 128)), 1)

    kinds = jnp.pad(species_table, ((0, 2), (0, 0)))
    w_kind = jnp.concatenate([*thirds(kinds), jnp.zeros((8, 128), f32)], axis=0).T.astype(bf16)
    rad_high, rad_low = halves(w_radial)
    w_pair = jnp.concatenate(
        [w_neigh.astype(f32), rad_high, rad_low, rad_high, jnp.zeros((8, 128), f32)], axis=0
    ).T.astype(bf16)
    w_rad = jnp.concatenate([rad_high, rad_low], axis=0).astype(bf16)
    w_ec = jnp.concatenate([w_env[0], w_tensor[0]], axis=1)
    w_back = jnp.concatenate([w_latent[0, :128], w_ec], axis=1)
    w_out_row = jnp.pad(w_out[None], ((0, 15), (0, 0)))
    cols = jnp.stack([charge_weight, w_out.astype(f32)], axis=1)
    operands = (
        blocks,
        neighbours[0, 0],
        counts[0],
        w_kind,
        w_pair,
        w_center.T,
        w_two.T,
        w_ec.T,
        w_latent[0].T,
        w_two,
        w_back,
        w_latent[0, 128:],
        w_rad,
        w_out_row,
        cols,
    )
    vmem = pl.BlockSpec(memory_space=pltpu.VMEM)
    grads, energy = pl.pallas_call(
        edge_kernel,
        out_shape=(
            jax.ShapeDtypeStruct((4, 16, 64), f32),
            jax.ShapeDtypeStruct((1, 64), f32),
        ),
        in_specs=[vmem] * len(operands),
        out_specs=(vmem, vmem),
        scratch_shapes=[
            pltpu.VMEM((128, 1024), f32),
            pltpu.VMEM((128, 1024), f32),
            pltpu.VMEM((128, 1024), f32),
            pltpu.VMEM((128, 1024), bf16),
            pltpu.VMEM((64, 1024), f32),
            pltpu.VMEM((64, 1024), f32),
            pltpu.VMEM((9, 64, 128), f32),
            pltpu.VMEM((3, 64, 1024), f32),
            pltpu.VMEM((128, 1024), bf16),
            pltpu.VMEM((64, 1024), bf16),
            pltpu.VMEM((9, 64, 128), f32),
            pltpu.VMEM((19, 8, 128), f32),
        ],
        compiler_params=pltpu.CompilerParams(vmem_limit_bytes=24 * 1024 * 1024),
        name="edges",
    )(*operands)
    back = jnp.sum(swap(grads, 0), axis=0).reshape(4, 4, 64)
    total = jnp.sum(swap(back, 1), axis=0)
    return (energy[None], -total[None, None, :3])


def solution(mesh):
    return jax.shard_map(
        local,
        mesh=mesh,
        in_specs=(
            P("gx", "yz", None, None),
            P("gx", "yz", None),
            P("gx", "yz", None),
            P("gx", "yz", None, None),
            P("gx", "yz", None),
            P("gx", "yz", None),
            P(),
            P(),
            P(),
            P(),
            P(),
            P(),
            P(),
            P(),
            P(),
            P(),
        ),
        out_specs=(P("gx", "yz", None), P("gx", "yz", None, None)),
        check_vma=False,
    )
```

time: 151 us -> 64.7 us (0.43)
  the two profiles are of different devices: /device:TPU:39 before, /device:TPU:1 now
where the time goes in v1:
time: 64.7 us; the launch traced here: 64 us
  starting transfers between devices  25.5 us (39%)
  blocking collectives  17.8 us (28%)
  local copies, waits for them, and re-layouts  11.2 us (17%)
  Pallas kernels  5.23 us (8%)
  other arithmetic  2.45 us (4%)
  waiting for transfers between devices  0.97 us (1%)
  between operations  0.81 us (1%)
    all_to_all x2, starting transfers between devices, swap(): lax.all_to_all(value, ('gx', 'yz'), 0, 0, axis_index_groups=groups_of(shi...  25.5 us
    all_to_all x2, blocking collectives, swap(): lax.all_to_all(value, ('gx', 'yz'), 0, 0, axis_index_groups=groups_of(shi...  17.8 us
    unnamed x39, local copies, waits for them, and re-layouts  8.15 us
    pallas_call x1, Pallas kernels, local(): pl.pallas_call(edge_kernel, out_shape=(jax.ShapeDtypeStruct((4, 16, 64),...  5.23 us
    all_to_all x2, other arithmetic, swap(): lax.all_to_all(value, ('gx', 'yz'), 0, 0, axis_index_groups=groups_of(shi...  1.35 us
  transfers between devices with their start and end apart: 2, of which 1 were waited for; matrix products, arithmetic and copies ran while one was open for 3% of the time, Pallas kernels for 0%

profile of v1, /device:TPU:1, one launch (start us, length us, event | category | flops | bytes accessed | tf_op | source)
XLA Modules:
  0.0 64.0 jit_solution(11558561790653278600)
XLA Ops:
  0.6 0.7 %copy.72 = f32[1,1,3,64]{3,2,1,0:T(4,128)S(1)} copy(f32[1,1,3,64]{3,1,2,0:T(1,128)} %param.16) | data formatting | bytes 1536
  1.4 0.7 %convert_bitcast_fusion.1 = f32[1,64]{1,0:T(1,128)S(1)} fusion(s32[1,1,64]{2,1,0:T(1,128)} %param.17), kind=kLoop, calls=%fused_computation.22 | loop fusion | flops 64 | bytes 512 | tf_op jit(solution)/shard_map/convert_element_type | solution.py:355
  2.0 0.7 %concatenate.25 = f32[8,64]{1,0:T(8,128)S(1)} concatenate(f32[3,64]{1,0:T(4,128)S(1)} %bitcast.48, f32[1,64]{1,0:T(1,128)} %bitcast.49, f32[1,64]{1,0:T(1,128)S(1)} %convert_bitcast_fusion.1, f32[1,64]{1,0:T(1,128)S(1)} %pad.12, f32[2,64]{1,0:T(2,128)S(1)} %broadcast_in_dim.23), dimensions={0} | concatenate | bytes 4096 | tf_op jit(solution)/shard_map/concatenate | solution.py:354
  2.8 0.6 broadcast_in_dim.24
  3.4 13.7 %all-to-all-start = ((f32[4,8,128]{2,1,0:T(8,128)}), f32[4,8,128]{2,1,0:T(8,128)S(1)}, u32[]{:S(2)}, u32[]{:S(2)}) async-start(f32[4,8,128]{2,1,0:T(8,128)} %broadcast_in_dim.24), calls=%async_computation | async-start | bytes 32768 | tf_op jit(solution)/shard_map/all_to_all | solution.py:27
  17.1 0.7 %copy-done.8 = f32[6,128]{1,0:T(8,128)S(1)} copy-done((f32[6,128]{1,0:T(8,128)S(1)}, f32[6,128]{1,0:T(8,128)}, u32[]{:S(2)}) %copy-start.8) | copy-done | bytes 3096
  17.8 0.1 copy.57
  18.0 0.6 copy-done.9
  18.7 0.1 copy.64
  18.8 0.6 copy-done.7
  19.5 0.5 copy-done.10
  20.3 0.6 broadcast_in_dim.26
  20.9 11.8 %all-to-all-start.1 = ((f32[4,32,128]{2,1,0:T(8,128)}), f32[4,32,128]{2,1,0:T(8,128)S(1)}, u32[]{:S(2)}, u32[]{:S(2)}) async-start(f32[4,32,128]{2,1,0:T(8,128)} %broadcast_in_dim.26), calls=%async_computation.1 | async-start | bytes 131072 | tf_op jit(solution)/shard_map/all_to_all | solution.py:27
  32.7 0.7 %copy-done.11 = f32[128]{0:T(128)S(1)} copy-done((f32[128]{0:T(128)S(1)}, f32[128]{0:T(128)}, u32[]{:S(2)}) %copy-start.11) | copy-done | bytes 536
  33.3 0.1 copy.59
  33.5 0.1 copy.60
  33.6 0.1 copy.66
  33.7 0.6 copy-done.4
  34.5 0.1 copy.67.w_ec_t_ref
  34.6 0.1 copy.68.cols_ref
  34.7 0.6 %copy-done.5 = bf16[128,128]{1,0:T(8,128)(2,1)S(1)} copy-done((bf16[128,128]{1,0:T(8,128)(2,1)S(1)}, bf16[128,128]{1,0:T(8,128)(2,1)}, u32[]{:S(2)}) %copy-start.5) | copy-done | bytes 32792
  35.5 0.6 %copy-done = bf16[128,128]{1,0:T(8,128)(2,1)S(1)} copy-done((bf16[128,128]{1,0:T(8,128)(2,1)S(1)}, bf16[128,128]{1,0:T(8,128)(2,1)}, u32[]{:S(2)}) %copy-start) | copy-done | bytes 32792
  36.3 0.1 concatenate.28
  36.5 1.0 %all-to-all-done.1.blocks_ref = f32[4,32,128]{2,1,0:T(8,128)S(1)} async-done(((f32[4,32,128]{2,1,0:T(8,128)}), f32[4,32,128]{2,1,0:T(8,128)S(1)}, u32[]{:S(2)}, u32[]{:S(2)}) %all-to-all-start.1) | async-done | bytes 65568 | tf_op jit(solution)/shard_map/all_to_all | solution.py:27
  37.5 0.7 %copy-done.2 = s32[1,1,64]{2,1,0:T(1,128)S(1)} copy-done((s32[1,1,64]{2,1,0:T(1,128)S(1)}, s32[1,1,64]{2,1,0:T(1,128)}, u32[]{:S(2)}) %copy-start.2) | copy-done | bytes 280
  38.1 5.2 %edges.1 = (f32[4,16,64]{2,1,0:T(8,128)S(1)}, f32[1,64]{1,0:T(1,128)}) custom-call(f32[4,32,128]{2,1,0:T(8,128)S(1)} %all-to-all-done.1.blocks_ref, s32[16,64]{1,0:T(8,128)S(1)} %bitcast.40, s32[1,64]{1,0:T(1,128)S(1)} %bitcast.41, bf16[128,32]{1,0:T(8,128)(2,1)S(1)} %maximum_bitcast_fusion.w_kind_ref, bf16[128,160]{1,0:T(8,128)(2,1)S(1)} %bitcast.37, ...), custom_call_target="tpu_custom_call" | custom-call | tf_op jit(solution)/shard_map/edges/pallas_call | solution.py:391
  43.4 7.2 %all_to_all.20 = f32[4,1,1024]{2,1,0:T(1,128)S(1)} all-to-all(f32[4,1,1024]{2,1,0:T(1,128)S(1)} %reshape.38), channel_id=1, replica_groups={{0,1,48,49},{2,3,50,51},{4,5,52,53},{6,7,54,55},{8,9,56,57},{10,11,58,5..., dimensions={0} | all-to-all | bytes 32768 | tf_op jit(solution)/shard_map/all_to_all | solution.py:27
  50.7 0.5 broadcast.15
  51.2 0.7 %reduce = f32[4,1024]{1,0:T(4,128)S(1)} reduce(f32[4,1,1024]{2,1,0:T(1,128)S(1)} %all_to_all.20, f32[]{:T(128)} %broadcast.15), dimensions={1}, to_apply=%all_to_all.14.reduce_sub_computation | reduce | bytes 32772 | tf_op jit(solution)/shard_map/all_to_all | solution.py:27
  52.0 10.6 %all_to_all.21 = f32[4,1,256]{2,1,0:T(1,128)S(1)} all-to-all(f32[4,1,256]{2,1,0:T(1,128)S(1)} %reshape.40), channel_id=1, replica_groups={{49,50,97,98},{51,52,99,100},{53,54,101,102},{55,56,103,104},{57,58,105..., dimensions={0} | all-to-all | bytes 8192 | tf_op jit(solution)/shard_map/all_to_all | solution.py:27
  62.6 0.7 %reduce.1 = f32[4,256]{1,0:T(4,128)S(1)} reduce(f32[4,1,256]{2,1,0:T(1,128)S(1)} %all_to_all.21, f32[]{:T(128)} %broadcast.15), dimensions={1}, to_apply=%all_to_all.15.reduce_sub_computation | reduce | bytes 8196 | tf_op jit(solution)/shard_map/all_to_all | solution.py:27
  63.4 0.6 copy.69
  (45 shorter events, 1.3 us)
Async XLA Ops:
  0.6 0.7 %copy-start.12 = (s32[1,1,56]{2,1,0:T(1,128)S(1)}, s32[1,1,56]{2,1,0:T(1,128)}, u32[]{:S(2)}) copy-start(s32[1,1,56]{2,1,0:T(1,128)} %param.21) | copy-start | bytes 676
  0.6 16.5 %copy-start.3 = (bf16[1,320,128]{2,1,0:T(8,128)(2,1)S(1)}, bf16[1,320,128]{2,1,0:T(8,128)(2,1)}, u32[]{:S(2)}) copy-start(bf16[1,320,128]{2,1,0:T(8,128)(2,1)} %param.30) | copy-start | bytes 245764
  3.4 16.9 %all-to-all-start = ((f32[4,8,128]{2,1,0:T(8,128)}), f32[4,8,128]{2,1,0:T(8,128)S(1)}, u32[]{:S(2)}, u32[]{:S(2)}) async-start(f32[4,8,128]{2,1,0:T(8,128)} %broadcast_in_dim.24), calls=%async_computation | async-start | bytes 32768 | tf_op jit(solution)/shard_map/all_to_all | solution.py:27
  17.1 0.7 %copy-start.8 = (f32[6,128]{1,0:T(8,128)S(1)}, f32[6,128]{1,0:T(8,128)}, u32[]{:S(2)}) copy-start(f32[6,128]{1,0:T(8,128)} %param.22) | copy-start | bytes 9220
  17.9 0.7 %copy-start.9 = (f32[8,128]{1,0:T(8,128)S(1)}, f32[8,128]{1,0:T(8,128)}, u32[]{:S(2)}) copy-start(f32[8,128]{1,0:T(8,128)} %param.26) | copy-start | bytes 12292
  17.9 0.7 %copy-start.6 = (bf16[1,128,64]{1,2,0:T(8,128)(2,1)S(1)}, bf16[1,128,64]{1,2,0:T(8,128)(2,1)}, u32[]{:S(2)}) copy-start(bf16[1,128,64]{1,2,0:T(8,128)(2,1)} %param.28) | copy-start | bytes 49156
  18.7 0.7 %copy-start.7 = (bf16[1,128,64]{1,2,0:T(8,128)(2,1)S(1)}, bf16[1,128,64]{1,2,0:T(8,128)(2,1)}, u32[]{:S(2)}) copy-start(bf16[1,128,64]{1,2,0:T(8,128)(2,1)} %param.29) | copy-start | bytes 49156
  19.4 0.7 %copy-start.10 = (bf16[128]{0:T(256)(128)(2,1)S(1)}, bf16[128]{0:T(256)(128)(2,1)}, u32[]{:S(2)}) copy-start(bf16[128]{0:T(256)(128)(2,1)} %param.31) | copy-start | bytes 772
  20.9 16.5 %all-to-all-start.1 = ((f32[4,32,128]{2,1,0:T(8,128)}), f32[4,32,128]{2,1,0:T(8,128)S(1)}, u32[]{:S(2)}, u32[]{:S(2)}) async-start(f32[4,32,128]{2,1,0:T(8,128)} %broadcast_in_dim.26), calls=%async_computation.1 | async-start | bytes 131072 | tf_op jit(solution)/shard_map/all_to_all | solution.py:27
  32.7 0.7 %copy-start.11 = (f32[128]{0:T(128)S(1)}, f32[128]{0:T(128)}, u32[]{:S(2)}) copy-start(f32[128]{0:T(128)} %param.23) | copy-start | bytes 1540
  33.6 0.8 %copy-start.4 = (bf16[128,128]{1,0:T(8,128)(2,1)S(1)}, bf16[128,128]{1,0:T(8,128)(2,1)}, u32[]{:S(2)}) copy-start(bf16[128,128]{1,0:T(8,128)(2,1)} %param.25) | copy-start | bytes 98308
  34.6 0.8 %copy-start.5 = (bf16[128,128]{1,0:T(8,128)(2,1)S(1)}, bf16[128,128]{1,0:T(8,128)(2,1)}, u32[]{:S(2)}) copy-start(bf16[128,128]{1,0:T(8,128)(2,1)} %param.24) | copy-start | bytes 98308
  35.4 0.8 %copy-start = (bf16[128,128]{1,0:T(8,128)(2,1)S(1)}, bf16[128,128]{1,0:T(8,128)(2,1)}, u32[]{:S(2)}) copy-start(bf16[128,128]{1,0:T(8,128)(2,1)} %w_two_ref.1) | copy-start | bytes 98308
  36.5 1.0 %copy-start.1 = (s32[1,1,16,64]{3,2,1,0:T(8,128)S(1)}, s32[1,1,16,64]{3,2,1,0:T(8,128)}, u32[]{:S(2)}) copy-start(s32[1,1,16,64]{3,2,1,0:T(8,128)} %param.19) | copy-start | bytes 12292
  37.4 0.7 %copy-start.2 = (s32[1,1,64]{2,1,0:T(1,128)S(1)}, s32[1,1,64]{2,1,0:T(1,128)}, u32[]{:S(2)}) copy-start(s32[1,1,64]{2,1,0:T(1,128)} %param.20) | copy-start | bytes 772

commit v2 on v1

--- a/solution.py
+++ b/solution.py
@@ -28,13 +28,12 @@
 
 
 def halves(value):
-    high = lax.reduce_precision(value, 8, 7)
-    return high, lax.reduce_precision(value - high, 8, 7)
-
-
-def thirds(value):
-    high, mid = halves(value)
-    return high, mid, lax.reduce_precision(value - high - mid, 8, 7)
+    high = value.astype(bf16).astype(f32)
+    return high, value - high
+
+
+def turned(value):
+    return value.astype(f32).T.astype(bf16)
 
 
 def mm(a, b):
@@ -47,24 +46,38 @@
 
 def sigmoid(x):
     return 0.5 * jnp.tanh(0.5 * x) + 0.5
+
+
+def pack_kernel(pos_ref, charge_ref, kind_ref, send_ref, out_ref):
+    out_ref[...] = jnp.zeros_like(out_ref)
+    for k in range(4):
+        for i in range(3):
+            out_ref[k, i : i + 1, 0:64] = pos_ref[i]
+        out_ref[k, 3:4, 0:64] = charge_ref[...]
+        out_ref[k, 4:5, 0:64] = kind_ref[...].astype(f32)
+        out_ref[k, 5:6, 0:56] = send_ref[...].astype(f32)
+
+
+def force_kernel(parts_ref, out_ref):
+    total = parts_ref[0] + parts_ref[1] + parts_ref[2] + parts_ref[3]
+    for i in range(3):
+        out_ref[i] = -total[i : i + 1, 0:64]
 
 
 def edge_kernel(
     blocks_ref,
     nb_ref,
     count_ref,
-    w_kind_ref,
-    w_pair_ref,
-    w_center_t_ref,
-    w_two_t_ref,
-    w_ec_t_ref,
-    w_lat_t_ref,
+    kinds_ref,
+    charge_weight_ref,
+    w_center_ref,
+    w_neigh_ref,
+    w_radial_ref,
     w_two_ref,
-    w_back_ref,
-    w_scal_ref,
-    w_rad_ref,
-    w_out_row_ref,
-    cols_ref,
+    w_env_t_ref,
+    w_tensor_t_ref,
+    w_latent_ref,
+    w_out_ref,
     grad_ref,
     energy_ref,
     lat_ref,
@@ -79,7 +92,35 @@
     dch_ref,
     dsum_ref,
     rows_ref,
+    kinds8_ref,
 ):
+    kinds8_ref[...] = jnp.zeros_like(kinds8_ref)
+    kinds8_ref[0:6, :] = kinds_ref[...]
+    kind_high, rest = halves(kinds8_ref[...])
+    kind_mid, kind_low = halves(rest)
+    rad_high, rad_low = halves(w_radial_ref[...])
+    none = jnp.zeros((8, 128), f32)
+    small = jnp.concatenate(
+        [rad_high, rad_low, rad_high, none, kind_high, kind_mid, kind_low, none, jnp.zeros((64, 128), f32)],
+        axis=0,
+    ).T.astype(bf16)
+    w_pair = jnp.concatenate([turned(w_neigh_ref[...]), small[:, 0:32]], axis=1)
+    w_kind = small[:, 32:64]
+    w_rad = jnp.concatenate([rad_high, rad_low], axis=0).astype(bf16)
+    w_center_t = turned(w_center_ref[...])
+    w_two_t = turned(w_two_ref[...])
+    w_lat_t = jnp.concatenate(
+        [turned(w_latent_ref[0:128, :]), turned(w_latent_ref[128:256, :]), turned(w_latent_ref[256:320, :])],
+        axis=1,
+    )
+    w_ec_t = jnp.concatenate([w_env_t_ref[...], w_tensor_t_ref[...]], axis=0)
+    w_back = jnp.concatenate([w_latent_ref[0:128, :], turned(w_ec_t)], axis=1)
+    w_scal = w_latent_ref[128:320, :]
+    w_out = w_out_ref[...].astype(f32)
+    w_out_row = jnp.broadcast_to(w_out, (16, 128)).astype(bf16)
+    cw = jnp.broadcast_to(charge_weight_ref[...], (128, 128)).T
+    wo = jnp.broadcast_to(w_out, (128, 128)).T
+
     odd_x = lax.rem(lax.axis_index("gx"), 2)
     odd_y = lax.rem(lax.axis_index("yz"), 2)
 
@@ -120,7 +161,7 @@
     far_x, far_y, far_z, far_q, far_s = [pick(i, atom, zero) for i in range(5)]
     step_x = jnp.where(blk >= 6, 1, jnp.where(blk >= 3, 0, -1))
     step_y = blk - 3 * (step_x + 1) - 1
-    mine = tables[4]
+    mine = half_turn(tables[4])
     off_x = far_x + box_side * step_x.astype(f32) - mine[0:1, :]
     off_y = far_y + box_side * step_y.astype(f32) - mine[1:2, :]
     off_z = far_z - mine[2:3, :]
@@ -142,8 +183,6 @@
     weight = jnp.exp(square * (-1.0 / 32.0)) * live
 
     kind_row = lax.broadcasted_iota(jnp.int32, (8, 128), 0).astype(f32)
-    cw = jnp.broadcast_to(cols_ref[:, 0:1], (128, 128))
-    wo = jnp.broadcast_to(cols_ref[:, 1:2], (128, 128))
     cw2 = jnp.concatenate([cw, cw], axis=1)
     wo2 = jnp.concatenate([wo, wo], axis=1)
     centres = 1.0 + lax.broadcasted_iota(jnp.int32, (8, 256), 0).astype(f32)
@@ -152,11 +191,11 @@
         onehot = jnp.where(kind == wide_row, 1.0, 0.0)
         pad = jnp.zeros_like(onehot)
         rhs = jnp.concatenate([onehot, onehot, onehot, pad], axis=0).astype(bf16)
-        mixed = mm(w_kind_ref[...], rhs) + wide_cw * charge
+        mixed = mm(w_kind, rhs) + wide_cw * charge
         return mixed * sigmoid(mixed)
 
     center = mm(
-        w_center_t_ref[...], hidden(mine[4:5, :], mine[3:4, :], cw, kind_row).astype(bf16)
+        w_center_t, hidden(mine[4:5, :], mine[3:4, :], cw, kind_row).astype(bf16)
     )
     center2 = jnp.concatenate([center, center], axis=1)
     kind_row2 = jnp.concatenate([kind_row, kind_row], axis=1)
@@ -174,18 +213,18 @@
         _, rb = basis(c)
         rb_high = rb.astype(bf16).astype(f32)
         rhs = jnp.concatenate([hid, rb_high, rb_high, rb - rb_high, jnp.zeros_like(rb)], axis=0)
-        pair = mm(w_pair_ref[...], rhs.astype(bf16)) + center2
+        pair = mm(w_pair, rhs.astype(bf16)) + center2
         sig = sigmoid(pair)
         act = pair * sig
         ds1_ref[:, at] = sig + act * (1.0 - sig)
-        second = mm(w_two_t_ref[...], act.astype(bf16))
+        second = mm(w_two_t, act.astype(bf16))
         sig = sigmoid(second)
         latent = second * sig
         ds2_ref[:, at] = sig + latent * (1.0 - sig)
         lat_ref[:, at] = latent
         latent_bf = latent.astype(bf16)
         lb_ref[:, at] = latent_bf
-        both = mm(w_ec_t_ref[...], latent_bf)
+        both = mm(w_ec_t, latent_bf)
         er_ref[:, at] = both[:64]
         ch_ref[:, at] = both[64:]
 
@@ -221,14 +260,14 @@
             grouped[g] = term if grouped[g] is None else grouped[g] + term
         scalars = [(g * channel).astype(bf16) for g in grouped]
         joined = jnp.concatenate([lb_ref[:, at]] + scalars, axis=0)
-        update = mm(w_lat_t_ref[...], joined)
+        update = mm(w_lat_t, joined)
         sig = sigmoid(update)
         act = update * sig
         out_bf = (lat_ref[:, at] + act).astype(bf16)
-        keep_row(0, c, mm(w_out_row_ref[...], out_bf)[0:1])
+        keep_row(0, c, mm(w_out_row, out_bf)[0:1])
         d_update = (wo2 * wide(weight, c) * (sig + act * (1.0 - sig))).astype(bf16)
         du_ref[:, at] = d_update
-        d_scal = mm(w_scal_ref[...], d_update)
+        d_scal = mm(w_scal, d_update)
         d_grouped = []
         d_channel = None
         for g in range(3):
@@ -264,13 +303,13 @@
         d_joined = jnp.concatenate(
             [du_ref[:, at], (d_env * w_row).astype(bf16), dch_ref[:, at]], axis=0
         )
-        d_latent = mm(w_back_ref[...], d_joined) + wo2 * w_row
+        d_latent = mm(w_back, d_joined) + wo2 * w_row
         d_second = (d_latent * ds2_ref[:, at]).astype(bf16)
         d_pair = mm(w_two_ref[...], d_second) * ds1_ref[:, at]
         high = d_pair.astype(bf16)
         low = (d_pair - high.astype(f32)).astype(bf16)
-        first = mm(w_rad_ref[...], high)
-        d_basis = first[0:8] + first[8:16] + mm(w_rad_ref[...], low)[0:8]
+        first = mm(w_rad, high)
+        d_basis = first[0:8] + first[8:16] + mm(w_rad, low)[0:8]
         spread, rb = basis(c)
         keep_row(18, c, jnp.sum(d_basis * rb * spread, axis=0, keepdims=True) * -4.0)
 
@@ -322,14 +361,11 @@
         + [jnp.zeros((1, 64), f32)],
         axis=0,
     )
-    near = jnp.concatenate([near, near], axis=0)
     home = ((1 + odd_x) // 2 * 2 + (1 + odd_y) // 2) * 4 + lax.rem(1 + odd_x, 2) * 2 + lax.rem(1 + odd_y, 2)
-    half_row = jnp.where(lax.broadcasted_iota(jnp.int32, (8, 64), 0) >= 4, 1, 0)
-    for i in range(8):
-        here = far[8 * i : 8 * i + 8]
-        grad_ref[i // 2, 8 * (i % 2) : 8 * (i % 2) + 8, :] = here - jnp.where(
-            half_row + 2 * i == home, near, 0.0
-        )
+    grad_ref[...] = jnp.zeros_like(grad_ref)
+    for i in range(16):
+        here = far[4 * i : 4 * i + 4] - jnp.where(home == i, near, 0.0)
+        grad_ref[i // 4, 8 * (i % 4) : 8 * (i % 4) + 4, 0:64] = here
 
 
 def local(
@@ -350,48 +386,35 @@
     w_latent,
     w_out,
 ):
-    sends = jnp.pad(send_list[0].astype(f32), ((0, 0), (0, 8)))
-    mine = jnp.concatenate(
-        [positions[0, 0], charges[0], species[0].astype(f32), sends, jnp.zeros((2, 64), f32)],
-        axis=0,
-    )
-    mine = jnp.concatenate([mine, mine], axis=1)
-    four = swap(jnp.broadcast_to(mine[None], (4, 8, 128)), 0).reshape(32, 128)
+    vmem = pl.BlockSpec(memory_space=pltpu.VMEM)
+    first = pl.pallas_call(
+        pack_kernel,
+        out_shape=jax.ShapeDtypeStruct((4, 8, 128), f32),
+        in_specs=[vmem] * 4,
+        out_specs=vmem,
+        name="pack",
+    )(positions.reshape(3, 1, 64), charges[0], species[0], send_list[0])
+    four = swap(first, 0).reshape(32, 128)
     blocks = swap(jnp.broadcast_to(four[None], (4, 32, 128)), 1)
-
-    kinds = jnp.pad(species_table, ((0, 2), (0, 0)))
-    w_kind = jnp.concatenate([*thirds(kinds), jnp.zeros((8, 128), f32)], axis=0).T.astype(bf16)
-    rad_high, rad_low = halves(w_radial)
-    w_pair = jnp.concatenate(
-        [w_neigh.astype(f32), rad_high, rad_low, rad_high, jnp.zeros((8, 128), f32)], axis=0
-    ).T.astype(bf16)
-    w_rad = jnp.concatenate([rad_high, rad_low], axis=0).astype(bf16)
-    w_ec = jnp.concatenate([w_env[0], w_tensor[0]], axis=1)
-    w_back = jnp.concatenate([w_latent[0, :128], w_ec], axis=1)
-    w_out_row = jnp.pad(w_out[None], ((0, 15), (0, 0)))
-    cols = jnp.stack([charge_weight, w_out.astype(f32)], axis=1)
     operands = (
         blocks,
         neighbours[0, 0],
         counts[0],
-        w_kind,
-        w_pair,
-        w_center.T,
-        w_two.T,
-        w_ec.T,
-        w_latent[0].T,
+        species_table,
+        charge_weight[None],
+        w_center,
+        w_neigh,
+        w_radial,
         w_two,
-        w_back,
-        w_latent[0, 128:],
-        w_rad,
-        w_out_row,
-        cols,
-    )
-    vmem = pl.BlockSpec(memory_space=pltpu.VMEM)
+        w_env[0].T,
+        w_tensor[0].T,
+        w_latent[0],
+        w_out[None],
+    )
     grads, energy = pl.pallas_call(
         edge_kernel,
         out_shape=(
-            jax.ShapeDtypeStruct((4, 16, 64), f32),
+            jax.ShapeDtypeStruct((4, 32, 128), f32),
             jax.ShapeDtypeStruct((1, 64), f32),
         ),
         in_specs=[vmem] * len(operands),
@@ -409,13 +432,20 @@
             pltpu.VMEM((64, 1024), bf16),
             pltpu.VMEM((9, 64, 128), f32),
             pltpu.VMEM((19, 8, 128), f32),
+            pltpu.VMEM((8, 128), f32),
         ],
-        compiler_params=pltpu.CompilerParams(vmem_limit_bytes=24 * 1024 * 1024),
+        compiler_params=pltpu.CompilerParams(vmem_limit_bytes=16 * 1024 * 1024),
         name="edges",
     )(*operands)
-    back = jnp.sum(swap(grads, 0), axis=0).reshape(4, 4, 64)
-    total = jnp.sum(swap(back, 1), axis=0)
-    return (energy[None], -total[None, None, :3])
+    back = jnp.sum(swap(grads, 0), axis=0).reshape(4, 8, 128)
+    forces = pl.pallas_call(
+        force_kernel,
+        out_shape=jax.ShapeDtypeStruct((3, 1, 64), f32),
+        in_specs=[vmem],
+        out_specs=vmem,
+        name="forces",
+    )(swap(back, 1))
+    return (energy[None], forces.reshape(1, 1, 3, 64))
 
 
 def solution(mesh):

time: 64.7 us -> 60 us (0.927)
  blocking collectives: 17.8 us -> 50.1 us
  starting transfers between devices: 25.5 us -> 0 us
  local copies, waits for them, and re-layouts: 11.2 us -> 0.66 us
  Pallas kernels: 5.23 us -> 8.03 us
  other arithmetic: 2.45 us -> 0.01 us
  waiting for transfers between devices: 0.97 us -> 0 us
    all_to_all x2 -> x4, blocking collectives: 17.8 us -> 50.1 us  [swap(): lax.all_to_all(value, ('gx', 'yz'), 0, 0, axis_index_groups=groups_of(shi...]
    all_to_all x2 -> x0, starting transfers between devices: 25.5 us -> none  [swap(): lax.all_to_all(value, ('gx', 'yz'), 0, 0, axis_index_groups=groups_of(shi...]
    unnamed x39 -> x24, local copies, waits for them, and re-layouts: 8.15 us -> 0.66 us
    pallas_call x1 -> x3, Pallas kernels: 5.23 us -> 8.03 us  [the longest x1 5.42 us: local(): pl.pallas_call(edge_kernel, out_shape=(jax.ShapeDtypeStruct((4, 32, 128),...]
    all_to_all x2 -> x0, other arithmetic: 1.35 us -> none  [swap(): lax.all_to_all(value, ('gx', 'yz'), 0, 0, axis_index_groups=groups_of(shi...]
    all_to_all x2 -> x0, waiting for transfers between devices: 0.97 us -> none  [swap(): lax.all_to_all(value, ('gx', 'yz'), 0, 0, axis_index_groups=groups_of(shi...]
    concatenate x2 -> x0, local copies, waits for them, and re-layouts: 0.79 us -> none  [the longest x1 0.67 us: local(): jnp.concatenate([positions[0, 0], charges[0], species[0].astype(f32), sen...]
    convert_element_type x3 -> x0, other arithmetic: 0.76 us -> none  [the longest x1 0.66 us: local(): species[0].astype(f32)]
  transfers between devices with their start and end apart: 2 -> 0, of which waited for: 1 -> 0; matrix products, arithmetic and copies ran while one was open for 3% -> 0% of each run, Pallas kernels for 0% -> 0%
where the time goes in v2:
time: 60 us; the launch traced here: 59.5 us
  blocking collectives  50.1 us (84%)
  Pallas kernels  8.03 us (13%)
  between operations  0.74 us (1%)
  local copies, waits for them, and re-layouts  0.66 us (1%)
    all_to_all x4, blocking collectives, swap(): lax.all_to_all(value, ('gx', 'yz'), 0, 0, axis_index_groups=groups_of(shi...  50.1 us
    pallas_call x1, Pallas kernels, local(): pl.pallas_call(edge_kernel, out_shape=(jax.ShapeDtypeStruct((4, 32, 128),...  5.42 us
    pallas_call x1, Pallas kernels, local(): pl.pallas_call(pack_kernel, out_shape=jax.ShapeDtypeStruct((4, 8, 128), f...  1.32 us
    pallas_call x1, Pallas kernels, local(): pl.pallas_call(force_kernel, out_shape=jax.ShapeDtypeStruct((3, 1, 64), f...  1.28 us

profile of v2, /device:TPU:1, one launch (start us, length us, event | category | flops | bytes accessed | tf_op | source)
XLA Modules:
  0.0 59.5 jit_solution(9560244155564111643)
XLA Ops:
  0.6 1.3 %pack.1 = f32[4,8,128]{2,1,0:T(8,128)} custom-call(f32[3,1,64]{2,1,0:T(1,128)} %bitcast.30, f32[1,64]{1,0:T(1,128)} %bitcast.32, s32[1,64]{1,0:T(1,128)} %bitcast.33, s32[1,56]{1,0:T(1,128)} %bitcast.34), custom_call_target="tpu_custom_call" | custom-call | tf_op jit(solution)/shard_map/pack/pallas_call | solution.py:390
  2.0 0.0 copy-start.8
  2.0 0.0 copy-start.11
  2.0 17.0 %all_to_all.20 = f32[4,8,128]{2,1,0:T(8,128)S(1)} all-to-all(f32[4,8,128]{2,1,0:T(8,128)} %pack.1), channel_id=1, replica_groups={{0,1,48,49},{2,3,50,51},{4,5,52,53},{6,7,54,55},{8,9,56,57},{10,11,58,5..., dimensions={0} | all-to-all | bytes 32768 | tf_op jit(solution)/shard_map/all_to_all | solution.py:27
  18.9 0.0 copy-start.2
  18.9 0.0 copy-start.3
  18.9 0.0 copy-start.5
  19.0 0.0 copy-start
  19.0 0.0 copy-start.1
  19.0 0.0 copy-start.4
  19.0 15.2 %all_to_all.21.blocks_ref = f32[4,32,128]{2,1,0:T(8,128)S(1)} all-to-all(f32[4,32,128]{2,1,0:T(8,128)S(1)} %broadcast_in_dim.17), channel_id=1, replica_groups={{49,50,97,98},{51,52,99,100},{53,54,101,102},{55,56,103,104},{57,58,105..., dimensions={0} | all-to-all | bytes 131072 | tf_op jit(solution)/shard_map/all_to_all | solution.py:27
  34.1 0.0 copy-start.6
  34.1 0.0 copy-start.7
  34.2 0.0 copy-start.9
  34.2 0.0 copy-start.10
  34.2 0.0 copy-done.8
  34.2 0.0 copy-done.11
  34.2 0.0 copy-done.2
  34.2 0.0 copy-done.3
  34.2 0.0 copy-done.5
  34.2 0.0 copy-done
  34.2 0.0 copy-done.1
  34.2 0.0 copy-done.4
  34.2 0.6 %copy-done.6 = s32[1,1,16,64]{3,2,1,0:T(8,128)S(1)} copy-done((s32[1,1,16,64]{3,2,1,0:T(8,128)S(1)}, s32[1,1,16,64]{3,2,1,0:T(8,128)}, u32[]{:S(2)}) %copy-start.6) | copy-done | bytes 4120
  34.8 0.0 copy-done.7
  34.9 0.0 copy-done.9
  34.9 0.0 copy-done.10
  34.9 5.4 %edges.1 = (f32[4,32,128]{2,1,0:T(8,128)S(1)}, f32[1,64]{1,0:T(1,128)}) custom-call(f32[4,32,128]{2,1,0:T(8,128)S(1)} %all_to_all.21.blocks_ref, s32[16,64]{1,0:T(8,128)S(1)} %bitcast.24, s32[1,64]{1,0:T(1,128)S(1)} %bitcast.25, f32[6,128]{1,0:T(8,128)S(1)} %copy-done.7, f32[1,128]{1,0:T(1,128)S(1)} %bitcast.26, bf16[128,128]{1,0:T(8,128)(2,1)S(1)} %copy-done.1, ...), custom_call_target="tpu_custom_call" | custom-call | tf_op jit(solution)/shard_map/edges/pallas_call | solution.py:414
  40.3 7.2 %all_to_all.22 = f32[4,32,128]{2,1,0:T(8,128)S(1)} all-to-all(f32[4,32,128]{2,1,0:T(8,128)S(1)} %get-tuple-element.5), channel_id=1, replica_groups={{0,1,48,49},{2,3,50,51},{4,5,52,53},{6,7,54,55},{8,9,56,57},{10,11,58,5..., dimensions={0} | all-to-all | bytes 131072 | tf_op jit(solution)/shard_map/all_to_all | solution.py:27
  47.5 10.8 %all_to_all.23.parts_ref = f32[4,8,128]{2,1,0:T(8,128)} all-to-all(f32[4,8,128]{2,1,0:T(8,128)S(1)} %bitcast.28), channel_id=1, replica_groups={{49,50,97,98},{51,52,99,100},{53,54,101,102},{55,56,103,104},{57,58,105..., dimensions={0} | all-to-all | bytes 32768 | tf_op jit(solution)/shard_map/all_to_all | solution.py:27
  58.2 1.3 %forces.1 = f32[3,1,64]{2,1,0:T(1,128)} custom-call(f32[4,8,128]{2,1,0:T(8,128)} %all_to_all.23.parts_ref), custom_call_target="tpu_custom_call" | custom-call | tf_op jit(solution)/shard_map/forces/pallas_call | solution.py:441
  (2 shorter events, 0.0 us)
Async XLA Ops:
  2.0 32.2 %copy-start.8 = (f32[8,128]{1,0:T(8,128)S(1)}, f32[8,128]{1,0:T(8,128)}, u32[]{:S(2)}) copy-start(f32[8,128]{1,0:T(8,128)} %w_radial_ref.1) | copy-start | bytes 12292
  2.0 32.2 %copy-start.11 = (bf16[128]{0:T(256)(128)(2,1)S(1)}, bf16[128]{0:T(256)(128)(2,1)}, u32[]{:S(2)}) copy-start(bf16[128]{0:T(256)(128)(2,1)} %param.31) | copy-start | bytes 772
  18.9 15.2 %copy-start.2 = (bf16[128,128]{1,0:T(8,128)(2,1)S(1)}, bf16[128,128]{1,0:T(8,128)(2,1)}, u32[]{:S(2)}) copy-start(bf16[128,128]{1,0:T(8,128)(2,1)} %w_neigh_ref.1) | copy-start | bytes 98308
  18.9 15.3 %copy-start.3 = (bf16[128,128]{1,0:T(8,128)(2,1)S(1)}, bf16[128,128]{1,0:T(8,128)(2,1)}, u32[]{:S(2)}) copy-start(bf16[128,128]{1,0:T(8,128)(2,1)} %w_two_ref.1) | copy-start | bytes 98308
  18.9 15.3 %copy-start.5 = (bf16[1,128,64]{1,2,0:T(8,128)(2,1)S(1)}, bf16[1,128,64]{1,2,0:T(8,128)(2,1)}, u32[]{:S(2)}) copy-start(bf16[1,128,64]{1,2,0:T(8,128)(2,1)} %param.29) | copy-start | bytes 49156
  19.0 15.3 %copy-start = (bf16[1,320,128]{2,1,0:T(8,128)(2,1)S(1)}, bf16[1,320,128]{2,1,0:T(8,128)(2,1)}, u32[]{:S(2)}) copy-start(bf16[1,320,128]{2,1,0:T(8,128)(2,1)} %param.30) | copy-start | bytes 245764
  19.0 15.3 %copy-start.1 = (bf16[128,128]{1,0:T(8,128)(2,1)S(1)}, bf16[128,128]{1,0:T(8,128)(2,1)}, u32[]{:S(2)}) copy-start(bf16[128,128]{1,0:T(8,128)(2,1)} %w_center_ref.1) | copy-start | bytes 98308
  19.0 15.3 %copy-start.4 = (bf16[1,128,64]{1,2,0:T(8,128)(2,1)S(1)}, bf16[1,128,64]{1,2,0:T(8,128)(2,1)}, u32[]{:S(2)}) copy-start(bf16[1,128,64]{1,2,0:T(8,128)(2,1)} %param.28) | copy-start | bytes 49156
  34.1 0.7 %copy-start.6 = (s32[1,1,16,64]{3,2,1,0:T(8,128)S(1)}, s32[1,1,16,64]{3,2,1,0:T(8,128)}, u32[]{:S(2)}) copy-start(s32[1,1,16,64]{3,2,1,0:T(8,128)} %param.19) | copy-start | bytes 12292
  34.1 0.7 %copy-start.7 = (f32[6,128]{1,0:T(8,128)S(1)}, f32[6,128]{1,0:T(8,128)}, u32[]{:S(2)}) copy-start(f32[6,128]{1,0:T(8,128)} %kinds_ref.1) | copy-start | bytes 9220
  34.2 0.7 %copy-start.9 = (s32[1,1,64]{2,1,0:T(1,128)S(1)}, s32[1,1,64]{2,1,0:T(1,128)}, u32[]{:S(2)}) copy-start(s32[1,1,64]{2,1,0:T(1,128)} %param.20) | copy-start | bytes 772
  34.2 0.7 %copy-start.10 = (f32[128]{0:T(128)S(1)}, f32[128]{0:T(128)}, u32[]{:S(2)}) copy-start(f32[128]{0:T(128)} %param.23) | copy-start | bytes 1540

commit v3 on v2

--- a/solution.py
+++ b/solution.py
@@ -10,11 +10,15 @@
 bf16 = jnp.bfloat16
 
 
-def groups_of(shift):
+FORTH = ((0, 0), (1, 1))
+BACK = ((0, 0), (1, 1))
+
+
+def groups_of(pairing):
     slabs, columns = lax.axis_size("gx"), lax.axis_size("yz")
     return [
         [
-            (2 * m + shift + a) % slabs * columns + (2 * n + shift + b) % columns
+            (2 * m + pairing[0] + a) % slabs * columns + (2 * n + pairing[1] + b) % columns
             for a in (0, 1)
             for b in (0, 1)
         ]
@@ -23,8 +27,12 @@
     ]
 
 
-def swap(value, shift):
-    return lax.all_to_all(value, ("gx", "yz"), 0, 0, axis_index_groups=groups_of(shift))
+def swap(value, pairing):
+    return lax.all_to_all(value, ("gx", "yz"), 0, 0, axis_index_groups=groups_of(pairing))
+
+
+def centre_of(odd, outer):
+    return 2 - odd if outer else 1 + odd
 
 
 def halves(value):
@@ -48,7 +56,21 @@
     return 0.5 * jnp.tanh(0.5 * x) + 0.5
 
 
-def pack_kernel(pos_ref, charge_ref, kind_ref, send_ref, out_ref):
+def pack_kernel(
+    pos_ref,
+    charge_ref,
+    kind_ref,
+    send_ref,
+    nb_ref,
+    count_ref,
+    table_ref,
+    charge_weight_ref,
+    w_radial_ref,
+    w_out_ref,
+    out_ref,
+    whole_ref,
+    small_ref,
+):
     out_ref[...] = jnp.zeros_like(out_ref)
     for k in range(4):
         for i in range(3):
@@ -56,6 +78,13 @@
         out_ref[k, 3:4, 0:64] = charge_ref[...]
         out_ref[k, 4:5, 0:64] = kind_ref[...].astype(f32)
         out_ref[k, 5:6, 0:56] = send_ref[...].astype(f32)
+    whole_ref[0:16, :] = nb_ref[...]
+    whole_ref[16:17, :] = count_ref[...]
+    small_ref[0:8, :] = jnp.zeros((8, 128), f32)
+    small_ref[0:6, :] = table_ref[...]
+    small_ref[8:16, :] = w_radial_ref[...]
+    small_ref[16:17, :] = charge_weight_ref[...]
+    small_ref[17:18, :] = w_out_ref[...].astype(f32)
 
 
 def force_kernel(parts_ref, out_ref):
@@ -66,18 +95,14 @@
 
 def edge_kernel(
     blocks_ref,
-    nb_ref,
-    count_ref,
-    kinds_ref,
-    charge_weight_ref,
+    whole_ref,
+    small_ref,
     w_center_ref,
     w_neigh_ref,
-    w_radial_ref,
     w_two_ref,
     w_env_t_ref,
     w_tensor_t_ref,
     w_latent_ref,
-    w_out_ref,
     grad_ref,
     energy_ref,
     lat_ref,
@@ -92,49 +117,47 @@
     dch_ref,
     dsum_ref,
     rows_ref,
-    kinds8_ref,
 ):
-    kinds8_ref[...] = jnp.zeros_like(kinds8_ref)
-    kinds8_ref[0:6, :] = kinds_ref[...]
-    kind_high, rest = halves(kinds8_ref[...])
+    w_center_t = turned(w_center_ref[...])
+    w_neigh_t = turned(w_neigh_ref[...])
+    w_two_t = turned(w_two_ref[...])
+    w_lat_t = jnp.concatenate(
+        [turned(w_latent_ref[0:128, :]), turned(w_latent_ref[128:256, :]), turned(w_latent_ref[256:320, :])],
+        axis=1,
+    )
+    w_ec_t = jnp.concatenate([w_env_t_ref[...], w_tensor_t_ref[...]], axis=0)
+    w_back = jnp.concatenate([w_latent_ref[0:128, :], turned(w_ec_t)], axis=1)
+    w_scal = w_latent_ref[128:320, :]
+    w_out = small_ref[17:18, :]
+    w_out_row = jnp.broadcast_to(w_out, (16, 128)).astype(bf16)
+    wo = jnp.broadcast_to(w_out, (128, 128)).T
+    kind_high, rest = halves(small_ref[0:8, :])
     kind_mid, kind_low = halves(rest)
-    rad_high, rad_low = halves(w_radial_ref[...])
+    rad_high, rad_low = halves(small_ref[8:16, :])
     none = jnp.zeros((8, 128), f32)
     small = jnp.concatenate(
         [rad_high, rad_low, rad_high, none, kind_high, kind_mid, kind_low, none, jnp.zeros((64, 128), f32)],
         axis=0,
     ).T.astype(bf16)
-    w_pair = jnp.concatenate([turned(w_neigh_ref[...]), small[:, 0:32]], axis=1)
+    w_pair = jnp.concatenate([w_neigh_t, small[:, 0:32]], axis=1)
     w_kind = small[:, 32:64]
     w_rad = jnp.concatenate([rad_high, rad_low], axis=0).astype(bf16)
-    w_center_t = turned(w_center_ref[...])
-    w_two_t = turned(w_two_ref[...])
-    w_lat_t = jnp.concatenate(
-        [turned(w_latent_ref[0:128, :]), turned(w_latent_ref[128:256, :]), turned(w_latent_ref[256:320, :])],
-        axis=1,
-    )
-    w_ec_t = jnp.concatenate([w_env_t_ref[...], w_tensor_t_ref[...]], axis=0)
-    w_back = jnp.concatenate([w_latent_ref[0:128, :], turned(w_ec_t)], axis=1)
-    w_scal = w_latent_ref[128:320, :]
-    w_out = w_out_ref[...].astype(f32)
-    w_out_row = jnp.broadcast_to(w_out, (16, 128)).astype(bf16)
-    cw = jnp.broadcast_to(charge_weight_ref[...], (128, 128)).T
-    wo = jnp.broadcast_to(w_out, (128, 128)).T
+    cw = jnp.broadcast_to(small_ref[16:17, :], (128, 128)).T
 
     odd_x = lax.rem(lax.axis_index("gx"), 2)
     odd_y = lax.rem(lax.axis_index("yz"), 2)
 
     def block(b):
-        u = 2 - odd_x + (b // 3 - 1)
-        v = 2 - odd_y + (b % 3 - 1)
+        u = centre_of(odd_x, FORTH[1][0]) + (b // 3 - 1)
+        v = centre_of(odd_y, FORTH[1][1]) + (b % 3 - 1)
         far = (u // 2) * 2 + v // 2
         near = (u % 2) * 2 + v % 2
         return blocks_ref[far, pl.ds(pl.multiple_of(near * 8, 8), 8), :]
 
     tables = [block(b) for b in range(9)]
 
-    ids = jnp.concatenate([nb_ref[0:8, :], nb_ref[8:16, :]], axis=1)
-    count = jnp.concatenate([count_ref[...], count_ref[...]], axis=1)
+    ids = jnp.concatenate([whole_ref[0:8, :], whole_ref[8:16, :]], axis=1)
+    count = jnp.concatenate([whole_ref[16:17, :], whole_ref[16:17, :]], axis=1)
     row = lax.broadcasted_iota(jnp.int32, (8, 128), 0)
     lane = lax.broadcasted_iota(jnp.int32, (8, 128), 1)
     slot = row + jnp.where(lane >= 64, 8, 0)
@@ -329,8 +352,10 @@
     e_y = g_y * inv + d_dist * y
     e_z = g_z * inv + d_dist * z
 
-    u = 1 + odd_x + step_x
-    v = 1 + odd_y + step_y
+    home_u = centre_of(odd_x, BACK[0][0])
+    home_v = centre_of(odd_y, BACK[0][1])
+    u = home_u + step_x
+    v = home_v + step_y
     target = ((u // 2) * 2 + v // 2) * 4 + (u % 2) * 2 + v % 2
     atom_row = lax.broadcasted_iota(jnp.int32, (64, 128), 0)
     pairs_row = lax.broadcasted_iota(jnp.int32, (8, 128), 0)
@@ -361,57 +386,18 @@
         + [jnp.zeros((1, 64), f32)],
         axis=0,
     )
-    home = ((1 + odd_x) // 2 * 2 + (1 + odd_y) // 2) * 4 + lax.rem(1 + odd_x, 2) * 2 + lax.rem(1 + odd_y, 2)
+    home = (home_u // 2 * 2 + home_v // 2) * 4 + home_u % 2 * 2 + home_v % 2
     grad_ref[...] = jnp.zeros_like(grad_ref)
     for i in range(16):
         here = far[4 * i : 4 * i + 4] - jnp.where(home == i, near, 0.0)
         grad_ref[i // 4, 8 * (i % 4) : 8 * (i % 4) + 4, 0:64] = here
 
 
-def local(
-    positions,
-    species,
-    charges,
-    neighbours,
-    counts,
-    send_list,
-    species_table,
-    charge_weight,
-    w_center,
-    w_neigh,
-    w_radial,
-    w_two,
-    w_env,
-    w_tensor,
-    w_latent,
-    w_out,
-):
-    vmem = pl.BlockSpec(memory_space=pltpu.VMEM)
-    first = pl.pallas_call(
-        pack_kernel,
-        out_shape=jax.ShapeDtypeStruct((4, 8, 128), f32),
-        in_specs=[vmem] * 4,
-        out_specs=vmem,
-        name="pack",
-    )(positions.reshape(3, 1, 64), charges[0], species[0], send_list[0])
-    four = swap(first, 0).reshape(32, 128)
-    blocks = swap(jnp.broadcast_to(four[None], (4, 32, 128)), 1)
-    operands = (
-        blocks,
-        neighbours[0, 0],
-        counts[0],
-        species_table,
-        charge_weight[None],
-        w_center,
-        w_neigh,
-        w_radial,
-        w_two,
-        w_env[0].T,
-        w_tensor[0].T,
-        w_latent[0],
-        w_out[None],
-    )
-    grads, energy = pl.pallas_call(
+vmem = pl.BlockSpec(memory_space=pltpu.VMEM)
+
+
+def edges(*operands):
+    return pl.pallas_call(
         edge_kernel,
         out_shape=(
             jax.ShapeDtypeStruct((4, 32, 128), f32),
@@ -432,19 +418,75 @@
             pltpu.VMEM((64, 1024), bf16),
             pltpu.VMEM((9, 64, 128), f32),
             pltpu.VMEM((19, 8, 128), f32),
-            pltpu.VMEM((8, 128), f32),
         ],
         compiler_params=pltpu.CompilerParams(vmem_limit_bytes=16 * 1024 * 1024),
         name="edges",
     )(*operands)
-    back = jnp.sum(swap(grads, 0), axis=0).reshape(4, 8, 128)
+
+
+def local(
+    positions,
+    species,
+    charges,
+    neighbours,
+    counts,
+    send_list,
+    species_table,
+    charge_weight,
+    w_center,
+    w_neigh,
+    w_radial,
+    w_two,
+    w_env,
+    w_tensor,
+    w_latent,
+    w_out,
+):
+    first, whole, small = pl.pallas_call(
+        pack_kernel,
+        out_shape=(
+            jax.ShapeDtypeStruct((4, 8, 128), f32),
+            jax.ShapeDtypeStruct((24, 64), jnp.int32),
+            jax.ShapeDtypeStruct((24, 128), f32),
+        ),
+        in_specs=[vmem] * 10,
+        out_specs=(vmem, vmem, vmem),
+        compiler_params=pltpu.CompilerParams(vmem_limit_bytes=1024 * 1024),
+        name="pack",
+    )(
+        positions.reshape(3, 1, 64),
+        charges[0],
+        species[0],
+        send_list[0],
+        neighbours[0, 0],
+        counts[0],
+        species_table,
+        charge_weight[None],
+        w_radial,
+        w_out[None],
+    )
+    four = swap(first, FORTH[0]).reshape(32, 128)
+    blocks = swap(jnp.broadcast_to(four[None], (4, 32, 128)), FORTH[1])
+    grads, energy = edges(
+        blocks,
+        whole,
+        small,
+        w_center,
+        w_neigh,
+        w_two,
+        w_env[0].T,
+        w_tensor[0].T,
+        w_latent[0],
+    )
+    sums = jnp.sum(swap(grads, BACK[0]), axis=0).reshape(4, 8, 128)
     forces = pl.pallas_call(
         force_kernel,
         out_shape=jax.ShapeDtypeStruct((3, 1, 64), f32),
         in_specs=[vmem],
         out_specs=vmem,
+        compiler_params=pltpu.CompilerParams(vmem_limit_bytes=1024 * 1024),
         name="forces",
-    )(swap(back, 1))
+    )(swap(sums, BACK[1]))
     return (energy[None], forces.reshape(1, 1, 3, 64))
 
 

time: 60 us -> 59.8 us (level)
  local copies, waits for them, and re-layouts: 0.66 us -> 3.37 us
  Pallas kernels: 8.03 us -> 6 us
  blocking collectives: 50.1 us -> 49.3 us
    unnamed x24 -> x32, local copies, waits for them, and re-layouts: 0.66 us -> 3.37 us
    pallas_call x2, Pallas kernels: 6.74 us -> 5.44 us  [the longest x1 5.43 us: edges(): pl.pallas_call(edge_kernel, out_shape=(jax.ShapeDtypeStruct((4, 32, 128),...]
    all_to_all x4, blocking collectives: 50.1 us -> 49.3 us  [swap(): lax.all_to_all(value, ('gx', 'yz'), 0, 0, axis_index_groups=groups_of(pai...]
    pallas_call x1, Pallas kernels: 1.28 us -> 0.57 us  [local(): pl.pallas_call(force_kernel, out_shape=jax.ShapeDtypeStruct((3, 1, 64), f...]
where the time goes in v3:
time: 59.8 us; the launch traced here: 59.4 us
  blocking collectives  49.3 us (82%)
  Pallas kernels  6 us (10%)
  local copies, waits for them, and re-layouts  3.37 us (6%)
  between operations  0.75 us (1%)
    all_to_all x4, blocking collectives, swap(): lax.all_to_all(value, ('gx', 'yz'), 0, 0, axis_index_groups=groups_of(pai...  49.3 us
    pallas_call x1, Pallas kernels, edges(): pl.pallas_call(edge_kernel, out_shape=(jax.ShapeDtypeStruct((4, 32, 128),...  5.43 us
    unnamed x32, local copies, waits for them, and re-layouts  3.37 us

profile of v3, /device:TPU:1, one launch (start us, length us, event | category | flops | bytes accessed | tf_op | source)
XLA Modules:
  0.0 59.4 jit_solution(13115624177612342071)
XLA Ops:
  0.6 0.0 copy-start.6
  0.6 0.0 copy-start.7
  0.7 0.0 copy-start.9
  0.7 0.0 copy-start.10
  0.7 0.0 copy-start.11
  0.7 0.0 copy-start.12
  0.7 0.6 %copy-done.6 = s32[1,1,16,64]{3,2,1,0:T(8,128)S(1)} copy-done((s32[1,1,16,64]{3,2,1,0:T(8,128)S(1)}, s32[1,1,16,64]{3,2,1,0:T(8,128)}, u32[]{:S(2)}) %copy-start.6) | copy-done | bytes 4120
  1.3 0.0 copy-done.7
  1.3 0.0 copy-done.9
  1.3 0.0 copy-done.10
  1.3 0.0 copy-done.11
  1.4 0.0 copy-done.12
  1.4 0.0 copy-start.8
  1.4 0.7 %copy-done.8 = f32[8,128]{1,0:T(8,128)S(1)} copy-done((f32[8,128]{1,0:T(8,128)S(1)}, f32[8,128]{1,0:T(8,128)}, u32[]{:S(2)}) %copy-start.8) | copy-done | bytes 4120
  2.1 0.7 %copy-done.13 = s32[1,1,64]{2,1,0:T(1,128)S(1)} copy-done((s32[1,1,64]{2,1,0:T(1,128)S(1)}, s32[1,1,64]{2,1,0:T(1,128)}, u32[]{:S(2)}) %copy-start.13) | copy-done | bytes 280
  2.7 0.7 %copy-done.14 = f32[128]{0:T(128)S(1)} copy-done((f32[128]{0:T(128)S(1)}, f32[128]{0:T(128)}, u32[]{:S(2)}) %copy-start.14) | copy-done | bytes 536
  3.4 0.7 %copy-done.15 = bf16[128]{0:T(256)(128)(2,1)S(1)} copy-done((bf16[128]{0:T(256)(128)(2,1)S(1)}, bf16[128]{0:T(256)(128)(2,1)}, u32[]{:S(2)}) %copy-start.15) | copy-done | bytes 280
  4.0 16.0 %all_to_all.20 = f32[4,8,128]{2,1,0:T(8,128)S(1)} all-to-all(f32[4,8,128]{2,1,0:T(8,128)S(1)} %get-tuple-element.7), channel_id=1, replica_groups={{0,1,48,49},{2,3,50,51},{4,5,52,53},{6,7,54,55},{8,9,56,57},{10,11,58,5..., dimensions={0} | all-to-all | bytes 32768 | tf_op jit(solution)/shard_map/all_to_all | solution.py:31
  20.0 0.0 copy-start
  20.1 0.0 copy-start.1
  20.1 0.0 copy-start.4
  20.1 15.2 %all_to_all.21.blocks_ref = f32[4,32,128]{2,1,0:T(8,128)S(1)} all-to-all(f32[4,32,128]{2,1,0:T(8,128)S(1)} %broadcast_in_dim.19), channel_id=1, replica_groups={{49,50,97,98},{51,52,99,100},{53,54,101,102},{55,56,103,104},{57,58,105..., dimensions={0} | all-to-all | bytes 131072 | tf_op jit(solution)/shard_map/all_to_all | solution.py:31
  35.2 0.0 copy-done.2
  35.2 0.0 copy-done.3
  35.2 0.0 copy-done.5
  35.2 0.0 copy-done
  35.3 0.0 copy-done.1
  35.3 0.0 copy-done.4
  35.3 5.4 %edges.1 = (f32[4,32,128]{2,1,0:T(8,128)S(1)}, f32[1,64]{1,0:T(1,128)}) custom-call(f32[4,32,128]{2,1,0:T(8,128)S(1)} %all_to_all.21.blocks_ref, s32[24,64]{1,0:T(8,128)S(1)} %get-tuple-element.8.whole_ref, f32[24,128]{1,0:T(8,128)S(1)} %get-tuple-element.9.small_ref, bf16[128,128]{1,0:T(8,128)(2,1)S(1)} %copy-done.1, bf16[128,128]{1,0:T(8,128)(2,1)S(1)} %copy-done.2, ...), custom_call_target="tpu_custom_call" | custom-call | tf_op jit(solution)/shard_map/edges/pallas_call | solution.py:400
  40.7 7.5 %all_to_all.22 = f32[4,32,128]{2,1,0:T(8,128)S(1)} all-to-all(f32[4,32,128]{2,1,0:T(8,128)S(1)} %get-tuple-element.11), channel_id=1, replica_groups={{0,1,48,49},{2,3,50,51},{4,5,52,53},{6,7,54,55},{8,9,56,57},{10,11,58,5..., dimensions={0} | all-to-all | bytes 131072 | tf_op jit(solution)/shard_map/all_to_all | solution.py:31
  48.2 10.7 %all_to_all.23.parts_ref = f32[4,8,128]{2,1,0:T(8,128)S(1)} all-to-all(f32[4,8,128]{2,1,0:T(8,128)S(1)} %bitcast.32), channel_id=1, replica_groups={{49,50,97,98},{51,52,99,100},{53,54,101,102},{55,56,103,104},{57,58,105..., dimensions={0} | all-to-all | bytes 32768 | tf_op jit(solution)/shard_map/all_to_all | solution.py:31
  58.8 0.6 forces.1
  (9 shorter events, 0.0 us)
Async XLA Ops:
  0.6 0.7 %copy-start.6 = (s32[1,1,16,64]{3,2,1,0:T(8,128)S(1)}, s32[1,1,16,64]{3,2,1,0:T(8,128)}, u32[]{:S(2)}) copy-start(s32[1,1,16,64]{3,2,1,0:T(8,128)} %param.19) | copy-start | bytes 12292
  0.6 0.7 %copy-start.7 = (f32[6,128]{1,0:T(8,128)S(1)}, f32[6,128]{1,0:T(8,128)}, u32[]{:S(2)}) copy-start(f32[6,128]{1,0:T(8,128)} %table_ref.1) | copy-start | bytes 9220
  0.7 0.7 %copy-start.9 = (f32[1,1,3,64]{3,1,2,0:T(1,128)S(1)}, f32[1,1,3,64]{3,1,2,0:T(1,128)}, u32[]{:S(2)}) copy-start(f32[1,1,3,64]{3,1,2,0:T(1,128)} %param.16) | copy-start | bytes 2308
  0.7 0.7 %copy-start.10 = (f32[1,1,64]{2,1,0:T(1,128)S(1)}, f32[1,1,64]{2,1,0:T(1,128)}, u32[]{:S(2)}) copy-start(f32[1,1,64]{2,1,0:T(1,128)} %param.18) | copy-start | bytes 772
  0.7 0.7 %copy-start.11 = (s32[1,1,64]{2,1,0:T(1,128)S(1)}, s32[1,1,64]{2,1,0:T(1,128)}, u32[]{:S(2)}) copy-start(s32[1,1,64]{2,1,0:T(1,128)} %param.17) | copy-start | bytes 772
  0.7 0.7 %copy-start.12 = (s32[1,1,56]{2,1,0:T(1,128)S(1)}, s32[1,1,56]{2,1,0:T(1,128)}, u32[]{:S(2)}) copy-start(s32[1,1,56]{2,1,0:T(1,128)} %param.21) | copy-start | bytes 676
  1.4 0.7 %copy-start.8 = (f32[8,128]{1,0:T(8,128)S(1)}, f32[8,128]{1,0:T(8,128)}, u32[]{:S(2)}) copy-start(f32[8,128]{1,0:T(8,128)} %w_radial_ref.1) | copy-start | bytes 12292
  2.1 0.7 %copy-start.13 = (s32[1,1,64]{2,1,0:T(1,128)S(1)}, s32[1,1,64]{2,1,0:T(1,128)}, u32[]{:S(2)}) copy-start(s32[1,1,64]{2,1,0:T(1,128)} %param.20) | copy-start | bytes 772
  2.7 0.7 %copy-start.14 = (f32[128]{0:T(128)S(1)}, f32[128]{0:T(128)}, u32[]{:S(2)}) copy-start(f32[128]{0:T(128)} %param.23) | copy-start | bytes 1540
  3.4 0.7 %copy-start.15 = (bf16[128]{0:T(256)(128)(2,1)S(1)}, bf16[128]{0:T(256)(128)(2,1)}, u32[]{:S(2)}) copy-start(bf16[128]{0:T(256)(128)(2,1)} %param.31) | copy-start | bytes 772
  20.0 15.2 %copy-start.2 = (bf16[128,128]{1,0:T(8,128)(2,1)S(1)}, bf16[128,128]{1,0:T(8,128)(2,1)}, u32[]{:S(2)}) copy-start(bf16[128,128]{1,0:T(8,128)(2,1)} %w_neigh_ref.1) | copy-start | bytes 98308
  20.0 15.2 %copy-start.3 = (bf16[128,128]{1,0:T(8,128)(2,1)S(1)}, bf16[128,128]{1,0:T(8,128)(2,1)}, u32[]{:S(2)}) copy-start(bf16[128,128]{1,0:T(8,128)(2,1)} %w_two_ref.1) | copy-start | bytes 98308
  20.0 15.2 %copy-start.5 = (bf16[1,128,64]{1,2,0:T(8,128)(2,1)S(1)}, bf16[1,128,64]{1,2,0:T(8,128)(2,1)}, u32[]{:S(2)}) copy-start(bf16[1,128,64]{1,2,0:T(8,128)(2,1)} %param.29) | copy-start | bytes 49156
  20.0 15.2 %copy-start = (bf16[1,320,128]{2,1,0:T(8,128)(2,1)S(1)}, bf16[1,320,128]{2,1,0:T(8,128)(2,1)}, u32[]{:S(2)}) copy-start(bf16[1,320,128]{2,1,0:T(8,128)(2,1)} %param.30) | copy-start | bytes 245764
  20.1 15.2 %copy-start.1 = (bf16[128,128]{1,0:T(8,128)(2,1)S(1)}, bf16[128,128]{1,0:T(8,128)(2,1)}, u32[]{:S(2)}) copy-start(bf16[128,128]{1,0:T(8,128)(2,1)} %w_center_ref.1) | copy-start | bytes 98308
  20.1 15.2 %copy-start.4 = (bf16[1,128,64]{1,2,0:T(8,128)(2,1)S(1)}, bf16[1,128,64]{1,2,0:T(8,128)(2,1)}, u32[]{:S(2)}) copy-start(bf16[1,128,64]{1,2,0:T(8,128)(2,1)} %param.28) | copy-start | bytes 49156

commit v4 on v3

--- a/solution.py
+++ b/solution.py
@@ -48,6 +48,13 @@
     return jnp.dot(a, b, preferred_element_type=f32)
 
 
+span = 8
+
+
+def repeat(value, axis=1):
+    return jnp.concatenate([value] * span, axis=axis)
+
+
 def half_turn(x):
     return x + pltpu.roll(x, 64, 1)
 
@@ -56,21 +63,7 @@
     return 0.5 * jnp.tanh(0.5 * x) + 0.5
 
 
-def pack_kernel(
-    pos_ref,
-    charge_ref,
-    kind_ref,
-    send_ref,
-    nb_ref,
-    count_ref,
-    table_ref,
-    charge_weight_ref,
-    w_radial_ref,
-    w_out_ref,
-    out_ref,
-    whole_ref,
-    small_ref,
-):
+def pack_kernel(pos_ref, charge_ref, kind_ref, send_ref, out_ref):
     out_ref[...] = jnp.zeros_like(out_ref)
     for k in range(4):
         for i in range(3):
@@ -78,13 +71,13 @@
         out_ref[k, 3:4, 0:64] = charge_ref[...]
         out_ref[k, 4:5, 0:64] = kind_ref[...].astype(f32)
         out_ref[k, 5:6, 0:56] = send_ref[...].astype(f32)
+
+
+def spread_kernel(four_ref, nb_ref, count_ref, out_ref, whole_ref):
+    for k in range(4):
+        out_ref[k] = four_ref[...]
     whole_ref[0:16, :] = nb_ref[...]
     whole_ref[16:17, :] = count_ref[...]
-    small_ref[0:8, :] = jnp.zeros((8, 128), f32)
-    small_ref[0:6, :] = table_ref[...]
-    small_ref[8:16, :] = w_radial_ref[...]
-    small_ref[16:17, :] = charge_weight_ref[...]
-    small_ref[17:18, :] = w_out_ref[...].astype(f32)
 
 
 def force_kernel(parts_ref, out_ref):
@@ -96,13 +89,16 @@
 def edge_kernel(
     blocks_ref,
     whole_ref,
-    small_ref,
+    table_ref,
+    charge_weight_ref,
     w_center_ref,
     w_neigh_ref,
+    w_radial_ref,
     w_two_ref,
     w_env_t_ref,
     w_tensor_t_ref,
     w_latent_ref,
+    w_out_ref,
     grad_ref,
     energy_ref,
     lat_ref,
@@ -117,7 +113,10 @@
     dch_ref,
     dsum_ref,
     rows_ref,
+    table8_ref,
 ):
+    table8_ref[...] = jnp.zeros_like(table8_ref)
+    table8_ref[0:6, :] = table_ref[...]
     w_center_t = turned(w_center_ref[...])
     w_neigh_t = turned(w_neigh_ref[...])
     w_two_t = turned(w_two_ref[...])
@@ -128,12 +127,12 @@
     w_ec_t = jnp.concatenate([w_env_t_ref[...], w_tensor_t_ref[...]], axis=0)
     w_back = jnp.concatenate([w_latent_ref[0:128, :], turned(w_ec_t)], axis=1)
     w_scal = w_latent_ref[128:320, :]
-    w_out = small_ref[17:18, :]
+    w_out = w_out_ref[...].astype(f32)
     w_out_row = jnp.broadcast_to(w_out, (16, 128)).astype(bf16)
     wo = jnp.broadcast_to(w_out, (128, 128)).T
-    kind_high, rest = halves(small_ref[0:8, :])
+    kind_high, rest = halves(table8_ref[...])
     kind_mid, kind_low = halves(rest)
-    rad_high, rad_low = halves(small_ref[8:16, :])
+    rad_high, rad_low = halves(w_radial_ref[...])
     none = jnp.zeros((8, 128), f32)
     small = jnp.concatenate(
         [rad_high, rad_low, rad_high, none, kind_high, kind_mid, kind_low, none, jnp.zeros((64, 128), f32)],
@@ -142,7 +141,7 @@
     w_pair = jnp.concatenate([w_neigh_t, small[:, 0:32]], axis=1)
     w_kind = small[:, 32:64]
     w_rad = jnp.concatenate([rad_high, rad_low], axis=0).astype(bf16)
-    cw = jnp.broadcast_to(small_ref[16:17, :], (128, 128)).T
+    cw = jnp.broadcast_to(charge_weight_ref[...], (128, 128)).T
 
     odd_x = lax.rem(lax.axis_index("gx"), 2)
     odd_y = lax.rem(lax.axis_index("yz"), 2)
@@ -206,9 +205,9 @@
     weight = jnp.exp(square * (-1.0 / 32.0)) * live
 
     kind_row = lax.broadcasted_iota(jnp.int32, (8, 128), 0).astype(f32)
-    cw2 = jnp.concatenate([cw, cw], axis=1)
-    wo2 = jnp.concatenate([wo, wo], axis=1)
-    centres = 1.0 + lax.broadcasted_iota(jnp.int32, (8, 256), 0).astype(f32)
+    cw2 = repeat(cw)
+    wo2 = repeat(wo)
+    centres = 1.0 + lax.broadcasted_iota(jnp.int32, (8, 128 * span), 0).astype(f32)
 
     def hidden(kind, charge, wide_cw, wide_row):
         onehot = jnp.where(kind == wide_row, 1.0, 0.0)
@@ -220,18 +219,18 @@
     center = mm(
         w_center_t, hidden(mine[4:5, :], mine[3:4, :], cw, kind_row).astype(bf16)
     )
-    center2 = jnp.concatenate([center, center], axis=1)
-    kind_row2 = jnp.concatenate([kind_row, kind_row], axis=1)
+    center2 = repeat(center)
+    kind_row2 = repeat(kind_row)
 
     def wide(packed, c):
-        return jnp.concatenate([packed[2 * c : 2 * c + 1, :], packed[2 * c + 1 : 2 * c + 2, :]], axis=1)
+        return jnp.concatenate([packed[r : r + 1, :] for r in range(span * c, span * c + span)], axis=1)
 
     def basis(c):
         spread = wide(dist, c) - centres
         return spread, jnp.exp(-2.0 * spread * spread)
 
-    for c in range(4):
-        at = slice(256 * c, 256 * c + 256)
+    for c in range(8 // span):
+        at = slice(128 * span * c, 128 * span * (c + 1))
         hid = hidden(wide(far_s, c), wide(far_q, c), cw2, kind_row2)
         _, rb = basis(c)
         rb_high = rb.astype(bf16).astype(f32)
@@ -266,19 +265,16 @@
             total = total + er_ref[:, lanes(r)] * row_of(scale, r)
         s_ref[m] = 0.25 * half_turn(total)
 
-    def double(value):
-        return jnp.concatenate([value, value], axis=1)
-
     def keep_row(index, c, value):
-        rows_ref[index, 2 * c : 2 * c + 1, :] = value[:, :128]
-        rows_ref[index, 2 * c + 1 : 2 * c + 2, :] = value[:, 128:]
-
-    for c in range(4):
-        at = slice(256 * c, 256 * c + 256)
+        for i in range(span):
+            rows_ref[index, span * c + i : span * c + i + 1, :] = value[:, 128 * i : 128 * i + 128]
+
+    for c in range(8 // span):
+        at = slice(128 * span * c, 128 * span * (c + 1))
         channel = ch_ref[:, at]
-        grouped = [double(s_ref[0]), None, None]
+        grouped = [repeat(s_ref[0]), None, None]
         for m in range(1, 9):
-            term = double(s_ref[m]) * wide(harm[m], c)
+            term = repeat(s_ref[m]) * wide(harm[m], c)
             g = group_of[m]
             grouped[g] = term if grouped[g] is None else grouped[g] + term
         scalars = [(g * channel).astype(bf16) for g in grouped]
@@ -301,7 +297,7 @@
             dg_ref[g, :, at] = d_grouped[g]
         dch_ref[:, at] = d_channel.astype(bf16)
         for m in range(1, 9):
-            keep_row(m, c, jnp.sum(d_grouped[group_of[m]] * double(s_ref[m]), axis=0, keepdims=True))
+            keep_row(m, c, jnp.sum(d_grouped[group_of[m]] * repeat(s_ref[m]), axis=0, keepdims=True))
 
     for m in range(9):
         g = group_of[m]
@@ -313,13 +309,13 @@
             total = term if total is None else total + term
         dsum_ref[m] = 0.25 * half_turn(total)
 
-    for c in range(4):
-        at = slice(256 * c, 256 * c + 256)
+    for c in range(8 // span):
+        at = slice(128 * span * c, 128 * span * (c + 1))
         raw = er_ref[:, at]
         w_row = wide(weight, c)
-        d_env = double(dsum_ref[0])
+        d_env = repeat(dsum_ref[0])
         for m in range(1, 9):
-            back = double(dsum_ref[m])
+            back = repeat(dsum_ref[m])
             d_env = d_env + back * wide(harm[m], c)
             keep_row(8 + m, c, jnp.sum(raw * back, axis=0, keepdims=True))
         keep_row(17, c, jnp.sum(raw * d_env, axis=0, keepdims=True))
@@ -418,6 +414,7 @@
             pltpu.VMEM((64, 1024), bf16),
             pltpu.VMEM((9, 64, 128), f32),
             pltpu.VMEM((19, 8, 128), f32),
+            pltpu.VMEM((8, 128), f32),
         ],
         compiler_params=pltpu.CompilerParams(vmem_limit_bytes=16 * 1024 * 1024),
         name="edges",
@@ -442,41 +439,38 @@
     w_latent,
     w_out,
 ):
-    first, whole, small = pl.pallas_call(
+    first = pl.pallas_call(
         pack_kernel,
-        out_shape=(
-            jax.ShapeDtypeStruct((4, 8, 128), f32),
-            jax.ShapeDtypeStruct((24, 64), jnp.int32),
-            jax.ShapeDtypeStruct((24, 128), f32),
-        ),
-        in_specs=[vmem] * 10,
-        out_specs=(vmem, vmem, vmem),
+        out_shape=jax.ShapeDtypeStruct((4, 8, 128), f32),
+        in_specs=[vmem] * 4,
+        out_specs=vmem,
         compiler_params=pltpu.CompilerParams(vmem_limit_bytes=1024 * 1024),
         name="pack",
-    )(
-        positions.reshape(3, 1, 64),
-        charges[0],
-        species[0],
-        send_list[0],
-        neighbours[0, 0],
-        counts[0],
+    )(positions.reshape(3, 1, 64), charges[0], species[0], send_list[0])
+    second, whole = pl.pallas_call(
+        spread_kernel,
+        out_shape=(
+            jax.ShapeDtypeStruct((4, 32, 128), f32),
+            jax.ShapeDtypeStruct((24, 64), jnp.int32),
+        ),
+        in_specs=[vmem] * 3,
+        out_specs=(vmem, vmem),
+        compiler_params=pltpu.CompilerParams(vmem_limit_bytes=1024 * 1024),
+        name="spread",
+    )(swap(first, FORTH[0]).reshape(32, 128), neighbours[0, 0], counts[0])
+    grads, energy = edges(
+        swap(second, FORTH[1]),
+        whole,
         species_table,
         charge_weight[None],
-        w_radial,
-        w_out[None],
-    )
-    four = swap(first, FORTH[0]).reshape(32, 128)
-    blocks = swap(jnp.broadcast_to(four[None], (4, 32, 128)), FORTH[1])
-    grads, energy = edges(
-        blocks,
-        whole,
-        small,
         w_center,
         w_neigh,
+        w_radial,
         w_two,
         w_env[0].T,
         w_tensor[0].T,
         w_latent[0],
+        w_out[None],
     )
     sums = jnp.sum(swap(grads, BACK[0]), axis=0).reshape(4, 8, 128)
     forces = pl.pallas_call(

time: 59.8 us -> 56.5 us (0.945)
  local copies, waits for them, and re-layouts: 3.37 us -> 1.34 us
  Pallas kernels: 6 us -> 4.62 us
    unnamed x32, local copies, waits for them, and re-layouts: 3.37 us -> 1.34 us
    pallas_call x1, Pallas kernels: 5.43 us -> 4.03 us  [edges(): pl.pallas_call(edge_kernel, out_shape=(jax.ShapeDtypeStruct((4, 32, 128),...]
where the time goes in v4:
time: 56.5 us; the launch traced here: 56.1 us
  blocking collectives  49.4 us (87%)
  Pallas kernels  4.62 us (8%)
  local copies, waits for them, and re-layouts  1.34 us (2%)
  between operations  0.79 us (1%)
    all_to_all x4, blocking collectives, swap(): lax.all_to_all(value, ('gx', 'yz'), 0, 0, axis_index_groups=groups_of(pai...  49.4 us
    pallas_call x1, Pallas kernels, edges(): pl.pallas_call(edge_kernel, out_shape=(jax.ShapeDtypeStruct((4, 32, 128),...  4.03 us
    unnamed x32, local copies, waits for them, and re-layouts  1.34 us

profile of v4, /device:TPU:1, one launch (start us, length us, event | category | flops | bytes accessed | tf_op | source)
XLA Modules:
  0.0 56.1 jit_solution(2400581150103671746)
XLA Ops:
  0.6 0.0 copy-start.15
  0.6 0.0 copy-start.9
  0.7 0.0 copy-start.12
  0.7 0.0 copy-start.13
  0.7 0.0 copy-start.14
  0.7 0.0 copy-start.8
  0.7 0.6 %copy-done.9 = f32[1,1,3,64]{3,1,2,0:T(1,128)S(1)} copy-done((f32[1,1,3,64]{3,1,2,0:T(1,128)S(1)}, f32[1,1,3,64]{3,1,2,0:T(1,128)}, u32[]{:S(2)}) %copy-start.9) | copy-done | bytes 792
  1.3 0.0 copy-done.12
  1.3 0.0 copy-done.13
  1.3 0.0 copy-done.14
  1.4 0.0 copy-start.3
  1.4 16.1 %all_to_all.20 = f32[4,8,128]{2,1,0:T(8,128)S(1)} all-to-all(f32[4,8,128]{2,1,0:T(8,128)S(1)} %pack.1), channel_id=1, replica_groups={{0,1,48,49},{2,3,50,51},{4,5,52,53},{6,7,54,55},{8,9,56,57},{10,11,58,5..., dimensions={0} | all-to-all | bytes 32768 | tf_op jit(solution)/shard_map/all_to_all | solution.py:31
  17.5 0.0 copy-done.15
  17.5 0.0 copy-done.6
  17.5 0.0 copy-start.1
  17.5 0.0 copy-start.2
  17.5 0.0 copy-start.4
  17.6 15.2 %all_to_all.21.blocks_ref = f32[4,32,128]{2,1,0:T(8,128)S(1)} all-to-all(f32[4,32,128]{2,1,0:T(8,128)S(1)} %get-tuple-element.6), channel_id=1, replica_groups={{49,50,97,98},{51,52,99,100},{53,54,101,102},{55,56,103,104},{57,58,105..., dimensions={0} | all-to-all | bytes 131072 | tf_op jit(solution)/shard_map/all_to_all | solution.py:31
  32.7 0.0 copy-done.8
  32.7 0.0 copy-done.5
  32.7 0.0 copy-done.3
  32.7 0.0 copy-done
  32.8 0.0 copy-done.1
  32.8 0.0 copy-done.2
  32.8 0.0 copy-done.4
  32.8 0.6 %copy-done.7 = f32[6,128]{1,0:T(8,128)S(1)} copy-done((f32[6,128]{1,0:T(8,128)S(1)}, f32[6,128]{1,0:T(8,128)}, u32[]{:S(2)}) %copy-start.7) | copy-done | bytes 3096
  33.4 0.0 copy-done.10
  33.4 0.0 copy-done.11
  33.4 4.0 %edges.1 = (f32[4,32,128]{2,1,0:T(8,128)S(1)}, f32[1,64]{1,0:T(1,128)}) custom-call(f32[4,32,128]{2,1,0:T(8,128)S(1)} %all_to_all.21.blocks_ref, s32[24,64]{1,0:T(8,128)S(1)} %get-tuple-element.7.whole_ref, f32[6,128]{1,0:T(8,128)S(1)} %copy-done.7, f32[1,128]{1,0:T(1,128)S(1)} %bitcast.27, bf16[128,128]{1,0:T(8,128)(2,1)S(1)} %copy-done.1, ...), custom_call_target="tpu_custom_call" | custom-call | tf_op jit(solution)/shard_map/edges/pallas_call | solution.py:396
  37.4 7.5 %all_to_all.22 = f32[4,32,128]{2,1,0:T(8,128)S(1)} all-to-all(f32[4,32,128]{2,1,0:T(8,128)S(1)} %get-tuple-element.9), channel_id=1, replica_groups={{0,1,48,49},{2,3,50,51},{4,5,52,53},{6,7,54,55},{8,9,56,57},{10,11,58,5..., dimensions={0} | all-to-all | bytes 131072 | tf_op jit(solution)/shard_map/all_to_all | solution.py:31
  44.9 10.7 %all_to_all.23.parts_ref = f32[4,8,128]{2,1,0:T(8,128)S(1)} all-to-all(f32[4,8,128]{2,1,0:T(8,128)S(1)} %bitcast.33), channel_id=1, replica_groups={{49,50,97,98},{51,52,99,100},{53,54,101,102},{55,56,103,104},{57,58,105..., dimensions={0} | all-to-all | bytes 32768 | tf_op jit(solution)/shard_map/all_to_all | solution.py:31
  55.6 0.6 %forces.1 = f32[3,1,64]{2,1,0:T(1,128)} custom-call(f32[4,8,128]{2,1,0:T(8,128)S(1)} %all_to_all.23.parts_ref), custom_call_target="tpu_custom_call" | custom-call | tf_op jit(solution)/shard_map/forces/pallas_call | solution.py:476
  (9 shorter events, 0.0 us)
Async XLA Ops:
  0.6 16.9 %copy-start.15 = (s32[1,1,64]{2,1,0:T(1,128)S(1)}, s32[1,1,64]{2,1,0:T(1,128)}, u32[]{:S(2)}) copy-start(s32[1,1,64]{2,1,0:T(1,128)} %param.20) | copy-start | bytes 772
  0.6 0.7 %copy-start.9 = (f32[1,1,3,64]{3,1,2,0:T(1,128)S(1)}, f32[1,1,3,64]{3,1,2,0:T(1,128)}, u32[]{:S(2)}) copy-start(f32[1,1,3,64]{3,1,2,0:T(1,128)} %param.16) | copy-start | bytes 2308
  0.7 0.7 %copy-start.12 = (f32[1,1,64]{2,1,0:T(1,128)S(1)}, f32[1,1,64]{2,1,0:T(1,128)}, u32[]{:S(2)}) copy-start(f32[1,1,64]{2,1,0:T(1,128)} %param.18) | copy-start | bytes 772
  0.7 0.7 %copy-start.13 = (s32[1,1,64]{2,1,0:T(1,128)S(1)}, s32[1,1,64]{2,1,0:T(1,128)}, u32[]{:S(2)}) copy-start(s32[1,1,64]{2,1,0:T(1,128)} %param.17) | copy-start | bytes 772
  0.7 0.7 %copy-start.14 = (s32[1,1,56]{2,1,0:T(1,128)S(1)}, s32[1,1,56]{2,1,0:T(1,128)}, u32[]{:S(2)}) copy-start(s32[1,1,56]{2,1,0:T(1,128)} %param.21) | copy-start | bytes 676
  0.7 32.0 %copy-start.8 = (f32[8,128]{1,0:T(8,128)S(1)}, f32[8,128]{1,0:T(8,128)}, u32[]{:S(2)}) copy-start(f32[8,128]{1,0:T(8,128)} %w_radial_ref.1) | copy-start | bytes 12292
  1.4 16.2 %copy-start.6 = (s32[1,1,16,64]{3,2,1,0:T(8,128)S(1)}, s32[1,1,16,64]{3,2,1,0:T(8,128)}, u32[]{:S(2)}) copy-start(s32[1,1,16,64]{3,2,1,0:T(8,128)} %param.19) | copy-start | bytes 12292
  1.4 31.4 %copy-start.5 = (bf16[1,128,64]{1,2,0:T(8,128)(2,1)S(1)}, bf16[1,128,64]{1,2,0:T(8,128)(2,1)}, u32[]{:S(2)}) copy-start(bf16[1,128,64]{1,2,0:T(8,128)(2,1)} %param.29) | copy-start | bytes 49156
  1.4 31.4 %copy-start.3 = (bf16[128,128]{1,0:T(8,128)(2,1)S(1)}, bf16[128,128]{1,0:T(8,128)(2,1)}, u32[]{:S(2)}) copy-start(bf16[128,128]{1,0:T(8,128)(2,1)} %w_two_ref.1) | copy-start | bytes 98308
  17.5 15.2 %copy-start = (bf16[1,320,128]{2,1,0:T(8,128)(2,1)S(1)}, bf16[1,320,128]{2,1,0:T(8,128)(2,1)}, u32[]{:S(2)}) copy-start(bf16[1,320,128]{2,1,0:T(8,128)(2,1)} %param.30) | copy-start | bytes 245764
  17.5 15.2 %copy-start.1 = (bf16[128,128]{1,0:T(8,128)(2,1)S(1)}, bf16[128,128]{1,0:T(8,128)(2,1)}, u32[]{:S(2)}) copy-start(bf16[128,128]{1,0:T(8,128)(2,1)} %w_center_ref.1) | copy-start | bytes 98308
  17.5 15.2 %copy-start.2 = (bf16[128,128]{1,0:T(8,128)(2,1)S(1)}, bf16[128,128]{1,0:T(8,128)(2,1)}, u32[]{:S(2)}) copy-start(bf16[128,128]{1,0:T(8,128)(2,1)} %w_neigh_ref.1) | copy-start | bytes 98308
  17.5 15.2 %copy-start.4 = (bf16[1,128,64]{1,2,0:T(8,128)(2,1)S(1)}, bf16[1,128,64]{1,2,0:T(8,128)(2,1)}, u32[]{:S(2)}) copy-start(bf16[1,128,64]{1,2,0:T(8,128)(2,1)} %param.28) | copy-start | bytes 49156
  32.7 0.7 %copy-start.7 = (f32[6,128]{1,0:T(8,128)S(1)}, f32[6,128]{1,0:T(8,128)}, u32[]{:S(2)}) copy-start(f32[6,128]{1,0:T(8,128)} %table_ref.1) | copy-start | bytes 9220
  32.7 0.7 %copy-start.10 = (f32[128]{0:T(128)S(1)}, f32[128]{0:T(128)}, u32[]{:S(2)}) copy-start(f32[128]{0:T(128)} %param.23) | copy-start | bytes 1540
  32.7 0.7 %copy-start.11 = (bf16[128]{0:T(256)(128)(2,1)S(1)}, bf16[128]{0:T(256)(128)(2,1)}, u32[]{:S(2)}) copy-start(bf16[128]{0:T(256)(128)(2,1)} %param.31) | copy-start | bytes 772

commit v5 on v4

--- a/solution.py
+++ b/solution.py
@@ -65,12 +65,12 @@
 
 def pack_kernel(pos_ref, charge_ref, kind_ref, send_ref, out_ref):
     out_ref[...] = jnp.zeros_like(out_ref)
+    code = (kind_ref[:, 0:56] + 8 * send_ref[...]).astype(f32)
     for k in range(4):
-        for i in range(3):
-            out_ref[k, i : i + 1, 0:64] = pos_ref[i]
-        out_ref[k, 3:4, 0:64] = charge_ref[...]
-        out_ref[k, 4:5, 0:64] = kind_ref[...].astype(f32)
-        out_ref[k, 5:6, 0:56] = send_ref[...].astype(f32)
+        out_ref[k, 0:1, :] = jnp.concatenate([pos_ref[0], pos_ref[1]], axis=1)
+        out_ref[k, 1:2, :] = jnp.concatenate([pos_ref[2], charge_ref[...]], axis=1)
+        out_ref[k, 2:3, 0:64] = kind_ref[...].astype(f32)
+        out_ref[k, 2:3, 0:56] = code
 
 
 def spread_kernel(four_ref, nb_ref, count_ref, out_ref, whole_ref):
@@ -82,8 +82,9 @@
 
 def force_kernel(parts_ref, out_ref):
     total = parts_ref[0] + parts_ref[1] + parts_ref[2] + parts_ref[3]
-    for i in range(3):
-        out_ref[i] = -total[i : i + 1, 0:64]
+    out_ref[0] = -total[0:1, 0:64]
+    out_ref[1] = -pltpu.roll(total, 64, 1)[0:1, 0:64]
+    out_ref[2] = -total[1:2, 0:64]
 
 
 def edge_kernel(
@@ -151,7 +152,7 @@
         v = centre_of(odd_y, FORTH[1][1]) + (b % 3 - 1)
         far = (u // 2) * 2 + v // 2
         near = (u % 2) * 2 + v % 2
-        return blocks_ref[far, pl.ds(pl.multiple_of(near * 8, 8), 8), :]
+        return [blocks_ref[far, pl.ds(near * 8 + i, 1), :] for i in range(3)]
 
     tables = [block(b) for b in range(9)]
 
@@ -172,21 +173,30 @@
     def pick(which, index, start):
         out = start
         for b in range(9):
-            table = jnp.broadcast_to(tables[b][which : which + 1, :], (8, 128))
+            table = jnp.broadcast_to(tables[b][which], (8, 128))
             value = jnp.take_along_axis(table, index, axis=1, mode="promise_in_bounds")
             out = jnp.where(blk == b, value, out)
         return out
 
-    listed = pick(5, place, jnp.zeros((8, 128), f32)).astype(jnp.int32)
+    zero = jnp.zeros((8, 128), f32)
+    listed = pick(2, place, zero).astype(jnp.int32) // 8
     atom = jnp.where(own, ids, listed)
-    zero = jnp.zeros((8, 128), f32)
-    far_x, far_y, far_z, far_q, far_s = [pick(i, atom, zero) for i in range(5)]
+    far_x = pick(0, atom, zero)
+    far_y = pick(0, atom + 64, zero)
+    far_z = pick(1, atom, zero)
+    far_q = pick(1, atom + 64, zero)
+    far_s = (pick(2, atom, zero).astype(jnp.int32) % 8).astype(f32)
     step_x = jnp.where(blk >= 6, 1, jnp.where(blk >= 3, 0, -1))
     step_y = blk - 3 * (step_x + 1) - 1
-    mine = half_turn(tables[4])
-    off_x = far_x + box_side * step_x.astype(f32) - mine[0:1, :]
-    off_y = far_y + box_side * step_y.astype(f32) - mine[1:2, :]
-    off_z = far_z - mine[2:3, :]
+    lower = lax.broadcasted_iota(jnp.int32, (1, 128), 1) < 64
+    mine = [(table, pltpu.roll(table, 64, 1)) for table in tables[4]]
+    (own_x, own_y), (own_z, own_q) = [
+        (jnp.where(lower, here, there), jnp.where(lower, there, here)) for here, there in mine[:2]
+    ]
+    own_s = (half_turn(tables[4][2]).astype(jnp.int32) % 8).astype(f32)
+    off_x = far_x + box_side * step_x.astype(f32) - own_x
+    off_y = far_y + box_side * step_y.astype(f32) - own_y
+    off_z = far_z - own_z
     square = off_x * off_x + off_y * off_y + off_z * off_z + 1.0
     dist = jnp.sqrt(square)
     inv = 1.0 / dist
@@ -217,7 +227,7 @@
         return mixed * sigmoid(mixed)
 
     center = mm(
-        w_center_t, hidden(mine[4:5, :], mine[3:4, :], cw, kind_row).astype(bf16)
+        w_center_t, hidden(own_s, own_q, cw, kind_row).astype(bf16)
     )
     center2 = repeat(center)
     kind_row2 = repeat(kind_row)
@@ -353,22 +363,15 @@
     u = home_u + step_x
     v = home_v + step_y
     target = ((u // 2) * 2 + v // 2) * 4 + (u % 2) * 2 + v % 2
-    atom_row = lax.broadcasted_iota(jnp.int32, (64, 128), 0)
-    pairs_row = lax.broadcasted_iota(jnp.int32, (8, 128), 0)
-    part_row = lax.rem(pairs_row, 4)
+    atom_row = lax.broadcasted_iota(jnp.int32, (128, 128), 0) % 64
+    target_row = lax.broadcasted_iota(jnp.int32, (16, 128), 0)
     left, right = [], []
     for r in range(8):
-        mixed = jnp.where(
-            part_row == 0,
-            row_of(e_x, r),
-            jnp.where(part_row == 1, row_of(e_y, r), jnp.where(part_row == 2, row_of(e_z, r), 0.0)),
-        )
-        high = mixed.astype(bf16).astype(f32)
-        low = mixed - high
-        goal = jnp.broadcast_to(row_of(target, r), (8, 128)) - jnp.where(pairs_row >= 4, 1, 0)
-        stack = [jnp.where(goal == 2 * i, high, 0.0) for i in range(8)]
-        stack += [jnp.where(goal == 2 * i, low, 0.0) for i in range(8)]
-        left.append(jnp.concatenate(stack, axis=0).astype(bf16))
+        here = target_row == row_of(target, r)
+        stack = [jnp.where(here, row_of(e, r), 0.0) for e in (e_x, e_y, e_z)]
+        high = [e.astype(bf16).astype(f32) for e in stack]
+        low = [e - h for e, h in zip(stack, high)]
+        left.append(jnp.concatenate(high + low, axis=0).astype(bf16))
         right.append(jnp.where(atom_row == row_of(atom, r), 1.0, 0.0).astype(bf16))
     far = lax.dot_general(
         jnp.concatenate(left, axis=1),
@@ -376,17 +379,18 @@
         (((1,), (1,)), ((), ())),
         preferred_element_type=f32,
     )
-    far = far[:64] + far[64:]
-    near = jnp.concatenate(
-        [half_turn(jnp.sum(e, axis=0, keepdims=True))[:, :64] for e in (e_x, e_y, e_z)]
-        + [jnp.zeros((1, 64), f32)],
-        axis=0,
-    )
+    far = far[:48] + far[48:]
     home = (home_u // 2 * 2 + home_v // 2) * 4 + home_u % 2 * 2 + home_v % 2
-    grad_ref[...] = jnp.zeros_like(grad_ref)
+    near = [half_turn(jnp.sum(e, axis=0, keepdims=True)) for e in (e_x, e_y, e_z)]
+    to_x, to_y, to_z = [
+        far[16 * i : 16 * i + 16] - jnp.where(target_row == home, near[i], 0.0) for i in range(3)
+    ]
+    first = jnp.where(lower, to_x, to_y)
+    second = jnp.where(lower, to_z, 0.0)
     for i in range(16):
-        here = far[4 * i : 4 * i + 4] - jnp.where(home == i, near, 0.0)
-        grad_ref[i // 4, 8 * (i % 4) : 8 * (i % 4) + 4, 0:64] = here
+        row = i % 4 * 2
+        grad_ref[i // 4, row : row + 1, :] = first[i : i + 1]
+        grad_ref[i // 4, row + 1 : row + 2, :] = second[i : i + 1]
 
 
 vmem = pl.BlockSpec(memory_space=pltpu.VMEM)
@@ -396,7 +400,7 @@
     return pl.pallas_call(
         edge_kernel,
         out_shape=(
-            jax.ShapeDtypeStruct((4, 32, 128), f32),
+            jax.ShapeDtypeStruct((4, 8, 128), f32),
             jax.ShapeDtypeStruct((1, 64), f32),
         ),
         in_specs=[vmem] * len(operands),
@@ -472,7 +476,7 @@
         w_latent[0],
         w_out[None],
     )
-    sums = jnp.sum(swap(grads, BACK[0]), axis=0).reshape(4, 8, 128)
+    sums = jnp.sum(swap(grads, BACK[0]), axis=0).reshape(4, 2, 128)
     forces = pl.pallas_call(
         force_kernel,
         out_shape=jax.ShapeDtypeStruct((3, 1, 64), f32),

time: 56.5 us -> 56.4 us (level)
  no operation moved by 1% of the time
where the time goes in v5:
time: 56.4 us; the launch traced here: 56 us
  blocking collectives  49.1 us (87%)
  Pallas kernels  4.76 us (8%)
  local copies, waits for them, and re-layouts  1.33 us (2%)
  between operations  0.77 us (1%)
    all_to_all x4, blocking collectives, swap(): lax.all_to_all(value, ('gx', 'yz'), 0, 0, axis_index_groups=groups_of(pai...  49.1 us
    pallas_call x1, Pallas kernels, edges(): pl.pallas_call(edge_kernel, out_shape=(jax.ShapeDtypeStruct((4, 8, 128),...  4.04 us
    unnamed x32, local copies, waits for them, and re-layouts  1.33 us

profile of v5, /device:TPU:1, one launch (start us, length us, event | category | flops | bytes accessed | tf_op | source)
XLA Modules:
  0.0 56.0 jit_solution(257244820759877802)
XLA Ops:
  0.6 0.0 copy-start.15
  0.6 0.0 copy-start.9
  0.7 0.0 copy-start.12
  0.7 0.0 copy-start.13
  0.7 0.0 copy-start.14
  0.7 0.0 copy-start.8
  0.7 0.6 %copy-done.9 = f32[1,1,3,64]{3,1,2,0:T(1,128)S(1)} copy-done((f32[1,1,3,64]{3,1,2,0:T(1,128)S(1)}, f32[1,1,3,64]{3,1,2,0:T(1,128)}, u32[]{:S(2)}) %copy-start.9) | copy-done | bytes 792
  1.3 0.0 copy-done.12
  1.3 0.0 copy-done.13
  1.3 0.0 copy-done.14
  1.4 0.1 pack.1
  1.4 16.1 %all_to_all.20 = f32[4,8,128]{2,1,0:T(8,128)S(1)} all-to-all(f32[4,8,128]{2,1,0:T(8,128)S(1)} %pack.1), channel_id=1, replica_groups={{0,1,48,49},{2,3,50,51},{4,5,52,53},{6,7,54,55},{8,9,56,57},{10,11,58,5..., dimensions={0} | all-to-all | bytes 32768 | tf_op jit(solution)/shard_map/all_to_all | solution.py:31
  17.5 0.0 copy-done.15
  17.5 0.0 copy-done.6
  17.6 0.0 copy-start.1
  17.6 0.0 copy-start.2
  17.6 0.0 copy-start.4
  17.6 15.2 %all_to_all.21.blocks_ref = f32[4,32,128]{2,1,0:T(8,128)S(1)} all-to-all(f32[4,32,128]{2,1,0:T(8,128)S(1)} %get-tuple-element.6), channel_id=1, replica_groups={{49,50,97,98},{51,52,99,100},{53,54,101,102},{55,56,103,104},{57,58,105..., dimensions={0} | all-to-all | bytes 131072 | tf_op jit(solution)/shard_map/all_to_all | solution.py:31
  32.8 0.0 copy-done.8
  32.8 0.0 copy-done.5
  32.8 0.0 copy-done.3
  32.8 0.0 copy-done
  32.8 0.0 copy-done.1
  32.8 0.0 copy-done.2
  32.8 0.0 copy-done.4
  32.8 0.6 %copy-done.7 = f32[6,128]{1,0:T(8,128)S(1)} copy-done((f32[6,128]{1,0:T(8,128)S(1)}, f32[6,128]{1,0:T(8,128)}, u32[]{:S(2)}) %copy-start.7) | copy-done | bytes 3096
  33.4 0.0 copy-done.10
  33.4 0.0 copy-done.11
  33.4 4.0 %edges.1 = (f32[4,8,128]{2,1,0:T(8,128)S(1)}, f32[1,64]{1,0:T(1,128)}) custom-call(f32[4,32,128]{2,1,0:T(8,128)S(1)} %all_to_all.21.blocks_ref, s32[24,64]{1,0:T(8,128)S(1)} %get-tuple-element.7.whole_ref, f32[6,128]{1,0:T(8,128)S(1)} %copy-done.7, f32[1,128]{1,0:T(1,128)S(1)} %bitcast.27, bf16[128,128]{1,0:T(8,128)(2,1)S(1)} %copy-done.1, ...), custom_call_target="tpu_custom_call" | custom-call | tf_op jit(solution)/shard_map/edges/pallas_call | solution.py:400
  37.5 7.3 %all_to_all.22 = f32[4,8,128]{2,1,0:T(8,128)S(1)} all-to-all(f32[4,8,128]{2,1,0:T(8,128)S(1)} %get-tuple-element.9), channel_id=1, replica_groups={{0,1,48,49},{2,3,50,51},{4,5,52,53},{6,7,54,55},{8,9,56,57},{10,11,58,5..., dimensions={0} | all-to-all | bytes 32768 | tf_op jit(solution)/shard_map/all_to_all | solution.py:31
  44.8 10.6 %all_to_all.23.parts_ref = f32[4,2,128]{2,1,0:T(2,128)S(1)} all-to-all(f32[4,2,128]{2,1,0:T(2,128)S(1)} %bitcast.33), channel_id=1, replica_groups={{49,50,97,98},{51,52,99,100},{53,54,101,102},{55,56,103,104},{57,58,105..., dimensions={0} | all-to-all | bytes 8192 | tf_op jit(solution)/shard_map/all_to_all | solution.py:31
  55.4 0.6 %forces.1 = f32[3,1,64]{2,1,0:T(1,128)} custom-call(f32[4,2,128]{2,1,0:T(2,128)S(1)} %all_to_all.23.parts_ref), custom_call_target="tpu_custom_call" | custom-call | tf_op jit(solution)/shard_map/forces/pallas_call | solution.py:480
  (9 shorter events, 0.0 us)
Async XLA Ops:
  0.6 16.9 %copy-start.15 = (s32[1,1,64]{2,1,0:T(1,128)S(1)}, s32[1,1,64]{2,1,0:T(1,128)}, u32[]{:S(2)}) copy-start(s32[1,1,64]{2,1,0:T(1,128)} %param.20) | copy-start | bytes 772
  0.6 0.7 %copy-start.9 = (f32[1,1,3,64]{3,1,2,0:T(1,128)S(1)}, f32[1,1,3,64]{3,1,2,0:T(1,128)}, u32[]{:S(2)}) copy-start(f32[1,1,3,64]{3,1,2,0:T(1,128)} %param.16) | copy-start | bytes 2308
  0.7 0.7 %copy-start.12 = (f32[1,1,64]{2,1,0:T(1,128)S(1)}, f32[1,1,64]{2,1,0:T(1,128)}, u32[]{:S(2)}) copy-start(f32[1,1,64]{2,1,0:T(1,128)} %param.18) | copy-start | bytes 772
  0.7 0.7 %copy-start.13 = (s32[1,1,64]{2,1,0:T(1,128)S(1)}, s32[1,1,64]{2,1,0:T(1,128)}, u32[]{:S(2)}) copy-start(s32[1,1,64]{2,1,0:T(1,128)} %param.17) | copy-start | bytes 772
  0.7 0.7 %copy-start.14 = (s32[1,1,56]{2,1,0:T(1,128)S(1)}, s32[1,1,56]{2,1,0:T(1,128)}, u32[]{:S(2)}) copy-start(s32[1,1,56]{2,1,0:T(1,128)} %param.21) | copy-start | bytes 676
  0.7 32.1 %copy-start.8 = (f32[8,128]{1,0:T(8,128)S(1)}, f32[8,128]{1,0:T(8,128)}, u32[]{:S(2)}) copy-start(f32[8,128]{1,0:T(8,128)} %w_radial_ref.1) | copy-start | bytes 12292
  1.4 16.2 %copy-start.6 = (s32[1,1,16,64]{3,2,1,0:T(8,128)S(1)}, s32[1,1,16,64]{3,2,1,0:T(8,128)}, u32[]{:S(2)}) copy-start(s32[1,1,16,64]{3,2,1,0:T(8,128)} %param.19) | copy-start | bytes 12292
  1.4 31.4 %copy-start.5 = (bf16[1,128,64]{1,2,0:T(8,128)(2,1)S(1)}, bf16[1,128,64]{1,2,0:T(8,128)(2,1)}, u32[]{:S(2)}) copy-start(bf16[1,128,64]{1,2,0:T(8,128)(2,1)} %param.29) | copy-start | bytes 49156
  1.4 31.3 %copy-start.3 = (bf16[128,128]{1,0:T(8,128)(2,1)S(1)}, bf16[128,128]{1,0:T(8,128)(2,1)}, u32[]{:S(2)}) copy-start(bf16[128,128]{1,0:T(8,128)(2,1)} %w_two_ref.1) | copy-start | bytes 98308
  17.5 15.2 %copy-start = (bf16[1,320,128]{2,1,0:T(8,128)(2,1)S(1)}, bf16[1,320,128]{2,1,0:T(8,128)(2,1)}, u32[]{:S(2)}) copy-start(bf16[1,320,128]{2,1,0:T(8,128)(2,1)} %param.30) | copy-start | bytes 245764
  17.6 15.2 %copy-start.1 = (bf16[128,128]{1,0:T(8,128)(2,1)S(1)}, bf16[128,128]{1,0:T(8,128)(2,1)}, u32[]{:S(2)}) copy-start(bf16[128,128]{1,0:T(8,128)(2,1)} %w_center_ref.1) | copy-start | bytes 98308
  17.6 15.2 %copy-start.2 = (bf16[128,128]{1,0:T(8,128)(2,1)S(1)}, bf16[128,128]{1,0:T(8,128)(2,1)}, u32[]{:S(2)}) copy-start(bf16[128,128]{1,0:T(8,128)(2,1)} %w_neigh_ref.1) | copy-start | bytes 98308
  17.6 15.2 %copy-start.4 = (bf16[1,128,64]{1,2,0:T(8,128)(2,1)S(1)}, bf16[1,128,64]{1,2,0:T(8,128)(2,1)}, u32[]{:S(2)}) copy-start(bf16[1,128,64]{1,2,0:T(8,128)(2,1)} %param.28) | copy-start | bytes 49156
  32.8 0.7 %copy-start.7 = (f32[6,128]{1,0:T(8,128)S(1)}, f32[6,128]{1,0:T(8,128)}, u32[]{:S(2)}) copy-start(f32[6,128]{1,0:T(8,128)} %table_ref.1) | copy-start | bytes 9220
  32.8 0.7 %copy-start.10 = (f32[128]{0:T(128)S(1)}, f32[128]{0:T(128)}, u32[]{:S(2)}) copy-start(f32[128]{0:T(128)} %param.23) | copy-start | bytes 1540
  32.8 0.7 %copy-start.11 = (bf16[128]{0:T(256)(128)(2,1)S(1)}, bf16[128]{0:T(256)(128)(2,1)}, u32[]{:S(2)}) copy-start(bf16[128]{0:T(256)(128)(2,1)} %param.31) | copy-start | bytes 772

commit v6 on v5

--- a/solution.py
+++ b/solution.py
@@ -59,8 +59,11 @@
     return x + pltpu.roll(x, 64, 1)
 
 
-def sigmoid(x):
-    return 0.5 * jnp.tanh(0.5 * x) + 0.5
+def gate(x):
+    half = 0.5 * x
+    turn = jnp.tanh(half)
+    act = half * turn + half
+    return act, 0.5 + 0.5 * (turn + act - act * turn)
 
 
 def pack_kernel(pos_ref, charge_ref, kind_ref, send_ref, out_ref):
@@ -121,16 +124,10 @@
     w_center_t = turned(w_center_ref[...])
     w_neigh_t = turned(w_neigh_ref[...])
     w_two_t = turned(w_two_ref[...])
-    w_lat_t = jnp.concatenate(
-        [turned(w_latent_ref[0:128, :]), turned(w_latent_ref[128:256, :]), turned(w_latent_ref[256:320, :])],
-        axis=1,
-    )
     w_ec_t = jnp.concatenate([w_env_t_ref[...], w_tensor_t_ref[...]], axis=0)
-    w_back = jnp.concatenate([w_latent_ref[0:128, :], turned(w_ec_t)], axis=1)
     w_scal = w_latent_ref[128:320, :]
     w_out = w_out_ref[...].astype(f32)
     w_out_row = jnp.broadcast_to(w_out, (16, 128)).astype(bf16)
-    wo = jnp.broadcast_to(w_out, (128, 128)).T
     kind_high, rest = halves(table8_ref[...])
     kind_mid, kind_low = halves(rest)
     rad_high, rad_low = halves(w_radial_ref[...])
@@ -216,7 +213,6 @@
 
     kind_row = lax.broadcasted_iota(jnp.int32, (8, 128), 0).astype(f32)
     cw2 = repeat(cw)
-    wo2 = repeat(wo)
     centres = 1.0 + lax.broadcasted_iota(jnp.int32, (8, 128 * span), 0).astype(f32)
 
     def hidden(kind, charge, wide_cw, wide_row):
@@ -224,7 +220,7 @@
         pad = jnp.zeros_like(onehot)
         rhs = jnp.concatenate([onehot, onehot, onehot, pad], axis=0).astype(bf16)
         mixed = mm(w_kind, rhs) + wide_cw * charge
-        return mixed * sigmoid(mixed)
+        return gate(mixed)[0]
 
     center = mm(
         w_center_t, hidden(own_s, own_q, cw, kind_row).astype(bf16)
@@ -246,19 +242,23 @@
         rb_high = rb.astype(bf16).astype(f32)
         rhs = jnp.concatenate([hid, rb_high, rb_high, rb - rb_high, jnp.zeros_like(rb)], axis=0)
         pair = mm(w_pair, rhs.astype(bf16)) + center2
-        sig = sigmoid(pair)
-        act = pair * sig
-        ds1_ref[:, at] = sig + act * (1.0 - sig)
+        act, ds1_ref[:, at] = gate(pair)
         second = mm(w_two_t, act.astype(bf16))
-        sig = sigmoid(second)
-        latent = second * sig
-        ds2_ref[:, at] = sig + latent * (1.0 - sig)
+        latent, ds2_ref[:, at] = gate(second)
         lat_ref[:, at] = latent
         latent_bf = latent.astype(bf16)
         lb_ref[:, at] = latent_bf
         both = mm(w_ec_t, latent_bf)
         er_ref[:, at] = both[:64]
         ch_ref[:, at] = both[64:]
+
+    w_lat_t = jnp.concatenate(
+        [turned(w_latent_ref[0:128, :]), turned(w_latent_ref[128:256, :]), turned(w_latent_ref[256:320, :])],
+        axis=1,
+    )
+    w_back = jnp.concatenate([w_latent_ref[0:128, :], turned(w_ec_t)], axis=1)
+    wo = jnp.broadcast_to(w_out, (128, 128)).T
+    wo2 = repeat(wo)
 
     def row_of(packed, r):
         return packed[r : r + 1, :]
@@ -290,11 +290,10 @@
         scalars = [(g * channel).astype(bf16) for g in grouped]
         joined = jnp.concatenate([lb_ref[:, at]] + scalars, axis=0)
         update = mm(w_lat_t, joined)
-        sig = sigmoid(update)
-        act = update * sig
+        act, slope = gate(update)
         out_bf = (lat_ref[:, at] + act).astype(bf16)
         keep_row(0, c, mm(w_out_row, out_bf)[0:1])
-        d_update = (wo2 * wide(weight, c) * (sig + act * (1.0 - sig))).astype(bf16)
+        d_update = (wo2 * wide(weight, c) * slope).astype(bf16)
         du_ref[:, at] = d_update
         d_scal = mm(w_scal, d_update)
         d_grouped = []

time: 56.4 us -> 56.5 us (level)
  no operation moved by 1% of the time
where the time goes in v6:
time: 56.5 us; the launch traced here: 56.1 us
  blocking collectives  49.1 us (87%)
  Pallas kernels  4.81 us (9%)
  local copies, waits for them, and re-layouts  1.33 us (2%)
  between operations  0.77 us (1%)
    all_to_all x4, blocking collectives, swap(): lax.all_to_all(value, ('gx', 'yz'), 0, 0, axis_index_groups=groups_of(pai...  49.1 us
    pallas_call x1, Pallas kernels, edges(): pl.pallas_call(edge_kernel, out_shape=(jax.ShapeDtypeStruct((4, 8, 128),...  4.1 us
    unnamed x32, local copies, waits for them, and re-layouts  1.33 us

profile of v6, /device:TPU:1, one launch (start us, length us, event | category | flops | bytes accessed | tf_op | source)
XLA Modules:
  0.0 56.1 jit_solution(12757425350256787658)
XLA Ops:
  0.6 0.0 copy-start.15
  0.6 0.0 copy-start.9
  0.7 0.0 copy-start.12
  0.7 0.0 copy-start.13
  0.7 0.0 copy-start.14
  0.7 0.0 copy-start.8
  0.7 0.6 %copy-done.9 = f32[1,1,3,64]{3,1,2,0:T(1,128)S(1)} copy-done((f32[1,1,3,64]{3,1,2,0:T(1,128)S(1)}, f32[1,1,3,64]{3,1,2,0:T(1,128)}, u32[]{:S(2)}) %copy-start.9) | copy-done | bytes 792
  1.3 0.0 copy-done.12
  1.3 0.0 copy-done.13
  1.3 0.0 copy-done.14
  1.4 0.1 pack.1
  1.4 16.1 %all_to_all.20 = f32[4,8,128]{2,1,0:T(8,128)S(1)} all-to-all(f32[4,8,128]{2,1,0:T(8,128)S(1)} %pack.1), channel_id=1, replica_groups={{0,1,48,49},{2,3,50,51},{4,5,52,53},{6,7,54,55},{8,9,56,57},{10,11,58,5..., dimensions={0} | all-to-all | bytes 32768 | tf_op jit(solution)/shard_map/all_to_all | solution.py:31
  17.5 0.0 copy-done.15
  17.5 0.0 copy-done.6
  17.6 0.0 copy-start.1
  17.6 0.0 copy-start.2
  17.6 0.0 copy-start.4
  17.6 15.2 %all_to_all.21.blocks_ref = f32[4,32,128]{2,1,0:T(8,128)S(1)} all-to-all(f32[4,32,128]{2,1,0:T(8,128)S(1)} %get-tuple-element.6), channel_id=1, replica_groups={{49,50,97,98},{51,52,99,100},{53,54,101,102},{55,56,103,104},{57,58,105..., dimensions={0} | all-to-all | bytes 131072 | tf_op jit(solution)/shard_map/all_to_all | solution.py:31
  32.8 0.0 copy-done.8
  32.8 0.0 copy-done.5
  32.8 0.0 copy-done.3
  32.8 0.0 copy-done
  32.8 0.0 copy-done.1
  32.8 0.0 copy-done.2
  32.8 0.0 copy-done.4
  32.8 0.6 %copy-done.7 = f32[6,128]{1,0:T(8,128)S(1)} copy-done((f32[6,128]{1,0:T(8,128)S(1)}, f32[6,128]{1,0:T(8,128)}, u32[]{:S(2)}) %copy-start.7) | copy-done | bytes 3096
  33.4 0.0 copy-done.10
  33.4 0.0 copy-done.11
  33.4 4.1 %edges.1 = (f32[4,8,128]{2,1,0:T(8,128)S(1)}, f32[1,64]{1,0:T(1,128)}) custom-call(f32[4,32,128]{2,1,0:T(8,128)S(1)} %all_to_all.21.blocks_ref, s32[24,64]{1,0:T(8,128)S(1)} %get-tuple-element.7.whole_ref, f32[6,128]{1,0:T(8,128)S(1)} %copy-done.7, f32[1,128]{1,0:T(1,128)S(1)} %bitcast.27, bf16[128,128]{1,0:T(8,128)(2,1)S(1)} %copy-done.1, ...), custom_call_target="tpu_custom_call" | custom-call | tf_op jit(solution)/shard_map/edges/pallas_call | solution.py:399
  37.5 7.3 %all_to_all.22 = f32[4,8,128]{2,1,0:T(8,128)S(1)} all-to-all(f32[4,8,128]{2,1,0:T(8,128)S(1)} %get-tuple-element.9), channel_id=1, replica_groups={{0,1,48,49},{2,3,50,51},{4,5,52,53},{6,7,54,55},{8,9,56,57},{10,11,58,5..., dimensions={0} | all-to-all | bytes 32768 | tf_op jit(solution)/shard_map/all_to_all | solution.py:31
  44.9 10.6 %all_to_all.23.parts_ref = f32[4,2,128]{2,1,0:T(2,128)S(1)} all-to-all(f32[4,2,128]{2,1,0:T(2,128)S(1)} %bitcast.33), channel_id=1, replica_groups={{49,50,97,98},{51,52,99,100},{53,54,101,102},{55,56,103,104},{57,58,105..., dimensions={0} | all-to-all | bytes 8192 | tf_op jit(solution)/shard_map/all_to_all | solution.py:31
  55.4 0.6 %forces.1 = f32[3,1,64]{2,1,0:T(1,128)} custom-call(f32[4,2,128]{2,1,0:T(2,128)S(1)} %all_to_all.23.parts_ref), custom_call_target="tpu_custom_call" | custom-call | tf_op jit(solution)/shard_map/forces/pallas_call | solution.py:479
  (9 shorter events, 0.0 us)
Async XLA Ops:
  0.6 16.9 %copy-start.15 = (s32[1,1,64]{2,1,0:T(1,128)S(1)}, s32[1,1,64]{2,1,0:T(1,128)}, u32[]{:S(2)}) copy-start(s32[1,1,64]{2,1,0:T(1,128)} %param.20) | copy-start | bytes 772
  0.6 0.7 %copy-start.9 = (f32[1,1,3,64]{3,1,2,0:T(1,128)S(1)}, f32[1,1,3,64]{3,1,2,0:T(1,128)}, u32[]{:S(2)}) copy-start(f32[1,1,3,64]{3,1,2,0:T(1,128)} %param.16) | copy-start | bytes 2308
  0.7 0.7 %copy-start.12 = (f32[1,1,64]{2,1,0:T(1,128)S(1)}, f32[1,1,64]{2,1,0:T(1,128)}, u32[]{:S(2)}) copy-start(f32[1,1,64]{2,1,0:T(1,128)} %param.18) | copy-start | bytes 772
  0.7 0.7 %copy-start.13 = (s32[1,1,64]{2,1,0:T(1,128)S(1)}, s32[1,1,64]{2,1,0:T(1,128)}, u32[]{:S(2)}) copy-start(s32[1,1,64]{2,1,0:T(1,128)} %param.17) | copy-start | bytes 772
  0.7 0.7 %copy-start.14 = (s32[1,1,56]{2,1,0:T(1,128)S(1)}, s32[1,1,56]{2,1,0:T(1,128)}, u32[]{:S(2)}) copy-start(s32[1,1,56]{2,1,0:T(1,128)} %param.21) | copy-start | bytes 676
  0.7 32.1 %copy-start.8 = (f32[8,128]{1,0:T(8,128)S(1)}, f32[8,128]{1,0:T(8,128)}, u32[]{:S(2)}) copy-start(f32[8,128]{1,0:T(8,128)} %w_radial_ref.1) | copy-start | bytes 12292
  1.4 16.2 %copy-start.6 = (s32[1,1,16,64]{3,2,1,0:T(8,128)S(1)}, s32[1,1,16,64]{3,2,1,0:T(8,128)}, u32[]{:S(2)}) copy-start(s32[1,1,16,64]{3,2,1,0:T(8,128)} %param.19) | copy-start | bytes 12292
  1.4 31.4 %copy-start.5 = (bf16[1,128,64]{1,2,0:T(8,128)(2,1)S(1)}, bf16[1,128,64]{1,2,0:T(8,128)(2,1)}, u32[]{:S(2)}) copy-start(bf16[1,128,64]{1,2,0:T(8,128)(2,1)} %param.29) | copy-start | bytes 49156
  1.4 31.3 %copy-start.3 = (bf16[128,128]{1,0:T(8,128)(2,1)S(1)}, bf16[128,128]{1,0:T(8,128)(2,1)}, u32[]{:S(2)}) copy-start(bf16[128,128]{1,0:T(8,128)(2,1)} %w_two_ref.1) | copy-start | bytes 98308
  17.5 15.2 %copy-start = (bf16[1,320,128]{2,1,0:T(8,128)(2,1)S(1)}, bf16[1,320,128]{2,1,0:T(8,128)(2,1)}, u32[]{:S(2)}) copy-start(bf16[1,320,128]{2,1,0:T(8,128)(2,1)} %param.30) | copy-start | bytes 245764
  17.6 15.2 %copy-start.1 = (bf16[128,128]{1,0:T(8,128)(2,1)S(1)}, bf16[128,128]{1,0:T(8,128)(2,1)}, u32[]{:S(2)}) copy-start(bf16[128,128]{1,0:T(8,128)(2,1)} %w_center_ref.1) | copy-start | bytes 98308
  17.6 15.2 %copy-start.2 = (bf16[128,128]{1,0:T(8,128)(2,1)S(1)}, bf16[128,128]{1,0:T(8,128)(2,1)}, u32[]{:S(2)}) copy-start(bf16[128,128]{1,0:T(8,128)(2,1)} %w_neigh_ref.1) | copy-start | bytes 98308
  17.6 15.2 %copy-start.4 = (bf16[1,128,64]{1,2,0:T(8,128)(2,1)S(1)}, bf16[1,128,64]{1,2,0:T(8,128)(2,1)}, u32[]{:S(2)}) copy-start(bf16[1,128,64]{1,2,0:T(8,128)(2,1)} %param.28) | copy-start | bytes 49156
  32.8 0.7 %copy-start.7 = (f32[6,128]{1,0:T(8,128)S(1)}, f32[6,128]{1,0:T(8,128)}, u32[]{:S(2)}) copy-start(f32[6,128]{1,0:T(8,128)} %table_ref.1) | copy-start | bytes 9220
  32.8 0.7 %copy-start.10 = (f32[128]{0:T(128)S(1)}, f32[128]{0:T(128)}, u32[]{:S(2)}) copy-start(f32[128]{0:T(128)} %param.23) | copy-start | bytes 1540
  32.8 0.7 %copy-start.11 = (bf16[128]{0:T(256)(128)(2,1)S(1)}, bf16[128]{0:T(256)(128)(2,1)}, u32[]{:S(2)}) copy-start(bf16[128]{0:T(256)(128)(2,1)} %param.31) | copy-start | bytes 772
